TPU v7x, 128 devices: a whole 4x4x4 slice. The times are simulated.
128 devices in a mesh: group: 32 (over x, z, core), expert: 4 (over y).
Axes of the slice: x: 4, y: 4, z: 4, core: 2. Of those that a mesh axis runs over, the one named last changes fastest.
Arguments:
- tokens: bfloat16 [16384, 1024], P(('group', 'expert')), may hold values from -6 to 6
- routes: int32 [1, 16384, 8], P(None, ('group', 'expert')), may hold values from 0 to 11, all different within a row
- slot_order: int32 [1, 128, 128], P(None, ('group', 'expert')), may hold values from 0 to 127, each once within a row
- prefix: int32 [32], P('group'), may hold values from 51 to 256
- attn_gain: float32 [1, 1024], replicated, may hold values from 0.5 to 1.5
- w_query: bfloat16 [1, 1024, 1024], replicated, may hold values from -0.25 to 0.25
- w_key: bfloat16 [1, 1024, 512], replicated, may hold values from -0.25 to 0.25
- w_value: bfloat16 [1, 1024, 512], replicated, may hold values from -0.1875 to 0.1875
- w_out: bfloat16 [1, 1024, 1024], replicated, may hold values from -0.75 to 0.75
- ffn_gain: float32 [1, 1024], replicated, may hold values from 0.5 to 1.5
- w_router: bfloat16 [1, 1024, 12], replicated, may hold values from -0.09375 to 0.09375
- w_gate: bfloat16 [1, 12, 1024, 512], P(None, 'expert'), may hold values from -0.1875 to 0.1875
- w_up: bfloat16 [1, 12, 1024, 512], P(None, 'expert'), may hold values from -0.1875 to 0.1875
- w_down: bfloat16 [1, 12, 512, 1024], P(None, 'expert'), may hold values from -0.5 to 0.5
- cotangent: float32 [16384, 1024], P(('group', 'expert')), may hold values from -6 to 6
Outputs:
- hidden_out: float32 [16384, 1024], P(('group', 'expert'))
- input_grad: float32 [16384, 1024], P(('group', 'expert'))
- grad_attn_gain: float32 [1, 1024], P(None, ('group', 'expert'))
- grad_query: float32 [1, 1024, 1024], P(None, ('group', 'expert'))
- grad_key: float32 [1, 1024, 512], P(None, ('group', 'expert'))
- grad_value: float32 [1, 1024, 512], P(None, ('group', 'expert'))
- grad_out: float32 [1, 1024, 1024], P(None, None, ('group', 'expert'))
- grad_ffn_gain: float32 [1, 1024], P(None, ('group', 'expert'))
- grad_router: float32 [1, 1024, 12], P(None, ('group', 'expert'))
- grad_gate: float32 [1, 12, 1024, 512], P(None, 'expert', 'group')
- grad_up: float32 [1, 12, 1024, 512], P(None, 'expert', 'group')
- grad_down: float32 [1, 12, 512, 1024], P(None, 'expert', None, 'group')
Inputs may be any that keep to these rules, and one draw needn't show every extreme that they name: `routes`: each row names 8 different experts. `slot_order`: each device's row of 128 entries in each layer is a permutation.
All inputs are finite; a program needn't handle non-finite values.
Results may differ from a plain program's by a relative error of at most 0.02.
Values may be sent and summed in bfloat16 or wider, within the bound.
A program may use at most 128 MiB of HBM per device.

v0:
```python
import jax
import jax.numpy as jnp
import numpy as np
from jax import lax
from jax.experimental import pallas as pl
from jax.experimental.pallas import tpu as pltpu
from jax.sharding import PartitionSpec as P

MESH = pl.DeviceIdType.MESH
LOW = jnp.bfloat16
F32 = jnp.float32
EPS = 1e-06
CAP = 96
EXPERTS = 12
OWN_EXPERTS = 3
EXPERT_UNITS = 9
UNITS = 15
WIDE = 512
KEY_UNIT, VALUE_UNIT, QUERY_UNIT, OUT_UNIT, SPARE = 9, 10, 11, 13, 15
BIG = (4, 4, 2, 32, WIDE)
KV, COT, CODE, ROWS, BACK, DOTS, MIX, KVG = range(8)


def group_of(x_at, z_at, core):
    return x_at * 8 + z_at * 2 + core


def dot(first, second):
    return jnp.dot(first, second, preferred_element_type=F32)


def dot_nt(first, second):
    return lax.dot_general(first, second, (((1,), (1,)), ((), ())), preferred_element_type=F32)


def dot_tn(first, second):
    return lax.dot_general(first, second, (((0,), (0,)), ((), ())), preferred_element_type=F32)


def sum32(first, second):
    return (first.astype(F32) + second.astype(F32)).astype(LOW)


def lanes_of(shape):
    return lax.broadcasted_iota(jnp.int32, shape, len(shape) - 1)


def turn(values, cosine, sine, sign):
    first = lanes_of((128, 128)) % 64 < 32
    parts = []
    for at in range(values.shape[1] // 128):
        part = values[:, at * 128 : at * 128 + 128]
        swapped = jnp.where(first, pltpu.roll(part, 96, 1), pltpu.roll(part, 32, 1))
        parts.append(part * cosine + sign * (swapped * sine))
    return parts[0] if len(parts) == 1 else jnp.concatenate(parts, axis=1)


def four_heads(first, second):
    low_half = lanes_of((128, 128)) < 64
    zero = jnp.zeros((128, 128), F32)
    return jnp.concatenate(
        [
            jnp.where(low_half, first, zero),
            jnp.where(low_half, pltpu.roll(first, 64, 1), zero),
            jnp.where(low_half, zero, pltpu.roll(second, 64, 1)),
            jnp.where(low_half, zero, second),
        ],
        axis=0,
    ).astype(LOW)


def unfold_heads(stood):
    first = jnp.concatenate([stood[0:64, 0:128], stood[0:64, 128:256]], axis=0)
    second = jnp.concatenate([stood[64:128, 256:384], stood[64:128, 384:512]], axis=0)
    return first.T, second.T


def loop(count, body):
    def step(index, carry):
        body(index)
        return carry

    lax.fori_loop(0, count, step, 0)


def lane_block(index, width=128):
    return pl.ds(pl.multiple_of(index * width, width), width)


def layer_kernel(
    tokens, routes, order, prefix, attn_gain, ffn_gain, w_router,
    wq_far, wk_far, wv_far, wo_far, wg_far, wu_far, wd_far, cot_far, cos_far, sin_far,
    hidden_out, input_grad, expert_out, shared_out, misc_out,
    grads, weights, wd, router, cot, cosine, sine,
    normed, normed_t, q_low, joined, q_four, kv_all, x_all, g_all, code_all,
    x_t, g_t, probs, gates, own_dots, dots_send, dots_in, row_send, row_in, mix_in, kvg_in,
    pair_in, lo_in, hi_in, minus_in, plus_in, lo_in_b, hi_in_b, minus_in_b, plus_in_b, last, last_in,
    misc, misc_pair, misc_lo, misc_hi, misc_minus, misc_plus, misc_lo_b, misc_hi_b, misc_minus_b, misc_plus_b,
    misc_last, misc_last_in,
    y_send, y_recv, send_sem, recv_sem, local_sem,
):
    middle, own_row = hidden_out, input_grad
    group = lax.axis_index("group")
    y_at = lax.axis_index("expert")
    x_at, z_at, core = group // 8, (group // 2) % 4, group % 2
    spots = (x_at, z_at)

    def device(axis, offset):
        if axis == 0:
            return (group_of((x_at + offset) % 4, z_at, core), y_at)
        return (group_of(x_at, (z_at + offset) % 4, core), y_at)

    def across(offset):
        return (group, (y_at + offset) % 4)

    partner = (group_of(x_at, z_at, 1 - core), y_at)
    barrier = pltpu.get_barrier_semaphore()
    peers = [partner] + [device(axis, off) for axis in (0, 1) for off in (1, 3)]
    peers += [across(off) for off in (1, 2, 3)]
    for peer in peers:
        pl.semaphore_signal(barrier, inc=1, device_id=peer, device_id_type=MESH)

    half = pl.ds(0, WIDE), pl.ds(WIDE, WIDE)
    loads = {}

    def load(name, src, dst):
        copy = pltpu.make_async_copy(src, dst, local_sem.at[len(loads)])
        loads[name] = copy
        copy.start()

    def attn_loads(tag, ref, order_of):
        wk_to, wv_to, wq_to, wo_to = order_of
        load((tag, 0), wk_far, ref.at[wk_to])
        load((tag, 1), wv_far, ref.at[wv_to])
        for part in (0, 1):
            load((tag, 2 + part), wq_far.at[:, :, :, :, half[part]], ref.at[wq_to + part])
        for part in (0, 1):
            load((tag, 4 + part), wo_far.at[:, :, :, :, half[part]], ref.at[wo_to + part])

    load("cos", cos_far.at[pl.ds(y_at * 128, 128)], cosine)
    load("sin", sin_far.at[pl.ds(y_at * 128, 128)], sine)
    attn_loads("fwd", grads, (0, 1, 2, 4))
    load("cot", cot_far, cot)
    load("wg", wg_far, weights.at[pl.ds(0, 3)])
    load("wu", wu_far, weights.at[pl.ds(3, 3)])
    load("wd", wd_far, wd)

    def square(ref, unit):
        return ref[unit].reshape(1024, WIDE)

    def slab(index, rows=None):
        unit, top = QUERY_UNIT + index // 2, (index % 2) * 2
        if rows is None:
            return grads.at[unit, pl.ds(top, 2)]
        kind, at = rows
        if kind == 256:
            return grads.at[unit, top + at]
        return grads.at[unit, top + at // 2, pl.ds((at % 2) * 2, 2)]

    hidden = tokens[...].astype(F32)
    attn_r = lax.rsqrt(jnp.mean(hidden * hidden, axis=1, keepdims=True) + EPS)
    normed[...] = (hidden * attn_r * attn_gain[...]).astype(LOW)
    for name in ("cos", "sin", ("fwd", 0), ("fwd", 1)):
        loads[name].wait()
    kv_all[y_at, :, 0:WIDE] = turn(dot(normed[...], square(grads, 0)), cosine[...], sine[...], 1.0).astype(LOW)
    kv_all[y_at, :, WIDE:] = dot(normed[...], square(grads, 1)).astype(LOW)
    pl.semaphore_wait(barrier, len(peers))

    def y_copy(kind, off, src, dst):
        return pltpu.make_async_remote_copy(
            src_ref=src, dst_ref=dst, send_sem=y_send.at[kind, off - 1], recv_sem=y_recv.at[kind, off - 1],
            device_id=across(off), device_id_type=MESH,
        )

    def share(kind, ref):
        return [y_copy(kind, off, ref.at[y_at], ref.at[y_at]) for off in (2, 1, 3)]

    def start(copies):
        for copy in copies:
            copy.start()

    def wait(copies):
        for copy in copies:
            copy.wait()

    kv_share = share(KV, kv_all)
    start(kv_share)

    for part in (0, 1):
        loads[("fwd", 2 + part)].wait()
        turned = turn(dot(normed[...], square(grads, 2 + part)), cosine[...], sine[...], 1.0)
        turned = turned.astype(LOW).astype(F32)
        for c in (0, 1):
            q_four[part * 2 + c] = four_heads(
                turned[:, c * 256 : c * 256 + 128], turned[:, c * 256 + 128 : c * 256 + 256]
            )

    lane = lanes_of((128, 128))
    member = jnp.zeros((128, 128), F32)
    for pick in range(routes.shape[1]):
        member = member + jnp.where(routes[:, pick : pick + 1] == lane, 1.0, 0.0)
    ranks = jnp.broadcast_to(order[...].astype(F32), (128, 128))
    earlier = jnp.where(ranks < ranks.T, 1.0, 0.0).astype(LOW)
    before = dot(earlier, member.astype(LOW))
    code_all[y_at] = jnp.where((member > 0.5) & (before < CAP - 0.5), 2.0, member).astype(LOW)
    loads["cot"].wait()
    g_all[y_at] = cot[...].astype(LOW)
    router[...] = jnp.zeros_like(router)
    router[:, 0:EXPERTS] = w_router[...]
    normed_t[...] = normed[...].T

    wait(kv_share)
    code_share = share(CODE, code_all)
    g_share = share(COT, g_all)
    start(code_share)
    start(g_share)

    def visible():
        shape = (512, 512)
        key_at = lax.broadcasted_iota(jnp.int32, shape, 0)
        query_at = y_at * 128 + lanes_of(shape) % 128
        return (key_at < prefix[0]) | (key_at <= query_at)

    def key_block(c):
        return kv_all[:, :, lane_block(c)].reshape(512, 128)

    def value_block(c):
        return kv_all[:, :, lane_block(c + 4)].reshape(512, 128)

    def prob_ref(c):
        return grads.at[KEY_UNIT + c // 2, pl.ds((c % 2) * 2, 2)]

    def attend(c):
        scores = jnp.where(visible(), dot_nt(key_block(c), q_four[c]) * 0.125, -1e30)
        raised = jnp.exp(scores - jnp.max(scores, axis=0, keepdims=True))
        soft = (raised * (1.0 / jnp.sum(raised, axis=0, keepdims=True))).astype(LOW)
        prob_ref(c)[...] = soft.reshape(2, 4, 2, 32, WIDE)
        first, second = unfold_heads(dot_tn(value_block(c), soft))
        joined[:, lane_block(2 * c)] = first.astype(LOW)
        joined[:, lane_block(2 * c + 1)] = second.astype(LOW)

    loop(4, attend)
    loads[("fwd", 4)].wait()
    loads[("fwd", 5)].wait()
    for part in (0, 1):
        middle[:, half[part]] = tokens[:, half[part]].astype(F32) + dot(joined[...], square(grads, 4 + part))
    ffn_r = lax.rsqrt(jnp.mean(middle[...] * middle[...], axis=1, keepdims=True) + EPS)
    x_all[y_at] = (middle[...] * ffn_r * ffn_gain[...]).astype(LOW)
    x_share = share(ROWS, x_all)
    start(x_share)

    wait(code_share)
    wait(g_share)

    def stand(ref, out):
        def body(block):
            out[:, lane_block(block)] = ref[block].T

        loop(4, body)

    stand(g_all, g_t)
    wait(x_share)
    stand(x_all, x_t)

    code = code_all[...].reshape(512, 128).astype(F32)
    in_use = code > 0.5
    logits = jnp.where(in_use, dot(x_all[...].reshape(512, 1024), router[...]), -1e30)
    raised = jnp.where(in_use, jnp.exp(logits - jnp.max(logits, axis=1, keepdims=True)), 0.0)
    soft = raised / jnp.sum(raised, axis=1, keepdims=True)
    probs[...] = soft.reshape(4, 128, 128)
    gates[...] = jnp.where(code > 1.5, soft, 0.0)
    own_dots[...] = jnp.zeros_like(own_dots)
    for name in ("wg", "wu", "wd"):
        loads[name].wait()

    def expert_step(step):
        j, part = step // 2, step % 2
        rows = pl.ds(pl.multiple_of(part * 256, 256), 256)
        blocks = pl.ds(part * 2, 2)
        here = lanes_of((256, 128)) == y_at * OWN_EXPERTS + j
        gate_of = jnp.sum(jnp.where(here, gates[rows, :], 0.0), axis=1, keepdims=True)
        inputs = x_all[blocks].reshape(256, 1024)
        gate_lin = dot(inputs, square(weights, j))
        up_lin = dot(inputs, square(weights, 3 + j))
        outer = dot_nt(g_all[blocks].reshape(256, 1024), wd[j])
        sig = 1.0 / (1.0 + jnp.exp(-gate_lin))
        silu = gate_lin * sig
        act = (silu * up_lin).astype(LOW).astype(F32)
        taken = jnp.where(gate_of > 0.0, jnp.sum(act * outer, axis=1, keepdims=True), 0.0)
        own_dots[rows, :] = jnp.where(here, taken, own_dots[rows, :])
        outer = outer * gate_of
        shape = (4, 2, 32, WIDE)
        slab(6 + j, (256, part))[...] = (act * gate_of).astype(LOW).reshape(shape)
        slab(j, (256, part))[...] = (outer * up_lin * sig * (1.0 + gate_lin * (1.0 - sig))).astype(LOW).reshape(shape)
        slab(3 + j, (256, part))[...] = (outer * silu).astype(LOW).reshape(shape)

    loop(6, expert_step)

    def dots_copy(off):
        return y_copy(DOTS, off, dots_send.at[(y_at + off) % 4], dots_in.at[off - 1])

    def back_copy(off):
        return y_copy(BACK, off, row_send.at[(y_at + off) % 4], row_in.at[off - 1])

    for block in range(4):
        dots_send[block] = own_dots[block * 128 : block * 128 + 128, :].T[0:16, :]
    for off in (2, 1, 3):
        dots_copy(off).start()

    def row_part(block):
        total = None
        for j in range(OWN_EXPERTS):
            for kind in (0, 3):
                lin = slab(kind + j, (128, block))[...].reshape(128, WIDE)
                part = dot_nt(lin, square(weights, kind + j))
                total = part if total is None else total + part
        return total

    for off in (2, 1, 3):
        row_send[(y_at + off) % 4] = row_part((y_at + off) % 4).astype(LOW)
        back_copy(off).start()
    own_row[...] = row_part(y_at)
    attn_loads("bwd", weights, (2, 5, 0, 3))

    class Wide:
        src, pair, lo, hi, minus, plus = grads, pair_in, lo_in, hi_in, minus_in, plus_in
        lo_b, hi_b, minus_b, plus_b = lo_in_b, hi_in_b, minus_in_b, plus_in_b

    class Narrow:
        src, pair, lo, hi, minus, plus = misc, misc_pair, misc_lo, misc_hi, misc_minus, misc_plus
        lo_b, hi_b, minus_b, plus_b = misc_lo_b, misc_hi_b, misc_minus_b, misc_plus_b

    def remote(unit, kind, src, dst, target):
        return pltpu.make_async_remote_copy(
            src_ref=src, dst_ref=dst, send_sem=send_sem.at[kind, unit], recv_sem=recv_sem.at[kind, unit],
            device_id=target, device_id_type=MESH,
        )

    class Unit:
        def __init__(self, unit):
            self.unit = unit
            self.set = Wide if unit < UNITS else Narrow
            self.at = unit if unit < UNITS else 0
            self.axis = unit % 2

        def block(self, axis, index):
            ref = self.set.src.at[self.at]
            return ref.at[index, :, core] if axis == 0 else ref.at[:, index, core]

        def cell(self, index):
            ref = self.set.src.at[self.at]
            return ref.at[x_at, index, core] if self.axis == 0 else ref.at[index, z_at, core]

        def pair_copy(self):
            s = self.set
            return remote(self.unit, 0, s.src.at[self.at, :, :, 1 - core], s.pair.at[self.at], partner)

        def far_copy(self, way):
            s = self.set
            src = self.block(self.axis, (spots[self.axis] + 2) % 4).at[pl.ds(2 * way, 2)]
            dst = (s.lo, s.hi)[way].at[self.at]
            return remote(self.unit, 1 + way, src, dst, device(self.axis, (1, 3)[way]))

        def near_copy(self, way):
            s = self.set
            src = self.block(self.axis, (spots[self.axis] + (1, 3)[way]) % 4)
            dst = (s.minus, s.plus)[way].at[self.at]
            return remote(self.unit, 3 + way, src, dst, device(self.axis, (1, 3)[way]))

        def far_copy_b(self, way):
            s = self.set
            src = self.cell((spots[1 - self.axis] + 2) % 4).at[pl.ds(16 * way, 16)]
            dst = (s.lo_b, s.hi_b)[way].at[self.at]
            return remote(self.unit, 5 + way, src, dst, device(1 - self.axis, (1, 3)[way]))

        def near_copy_b(self, way):
            s = self.set
            src = self.cell((spots[1 - self.axis] + (1, 3)[way]) % 4)
            dst = (s.minus_b, s.plus_b)[way].at[self.at]
            return remote(self.unit, 7 + way, src, dst, device(1 - self.axis, (1, 3)[way]))

        def across_copy(self, off):
            to = (y_at + off) % 4
            src, dst, at = (last, last_in, self.at - EXPERT_UNITS) if self.set is Wide else (misc_last, misc_last_in, 0)
            return remote(self.unit, 8 + off, src.at[at, pl.ds(to * 8, 8)], dst.at[off - 1, at], across(off))

        def begin(self):
            self.pair_copy().start()

        def after_pair(self):
            s = self.set
            self.pair_copy().wait()
            for slab_at in range(4):
                ref = s.src.at[self.at, slab_at, :, core]
                ref[...] = sum32(ref[...], s.pair[self.at, slab_at])
            self.far_copy(0).start()
            self.far_copy(1).start()

        def after_far(self):
            s = self.set
            for way in (0, 1):
                self.far_copy(way).wait()
                ref = self.block(self.axis, (spots[self.axis] + (1, 3)[way]) % 4).at[pl.ds(2 * way, 2)]
                ref[...] = sum32(ref[...], (s.lo, s.hi)[way][self.at])
                self.near_copy(way).start()

        def after_near(self):
            s = self.set
            for way in (0, 1):
                self.near_copy(way).wait()
            ref = self.block(self.axis, spots[self.axis])
            total = ref[...].astype(F32) + s.minus[self.at].astype(F32)
            ref[...] = (total + s.plus[self.at].astype(F32)).astype(LOW)
            for way in (0, 1):
                self.far_copy_b(way).start()

        def after_far_b(self):
            s = self.set
            for way in (0, 1):
                self.far_copy_b(way).wait()
                ref = self.cell((spots[1 - self.axis] + (1, 3)[way]) % 4).at[pl.ds(16 * way, 16)]
                ref[...] = sum32(ref[...], (s.lo_b, s.hi_b)[way][self.at])
                self.near_copy_b(way).start()

        def after_near_b(self):
            s = self.set
            for way in (0, 1):
                self.near_copy_b(way).wait()
            total = self.cell(spots[1 - self.axis])[...].astype(F32) + s.minus_b[self.at].astype(F32)
            total = total + s.plus_b[self.at].astype(F32)
            if self.unit < EXPERT_UNITS:
                expert_out[self.unit] = total
                return
            if self.set is Wide:
                last[self.at - EXPERT_UNITS] = total
            else:
                misc_last[0] = total
            for off in (1, 2, 3):
                self.across_copy(off).start()

        def finish(self):
            for off in (1, 2, 3):
                self.across_copy(off).wait()
            src, dst, at = (last, last_in, self.at - EXPERT_UNITS) if self.set is Wide else (misc_last, misc_last_in, 0)
            total = src[at, pl.ds(pl.multiple_of(y_at * 8, 8), 8), :]
            for off in (1, 2, 3):
                total = total + dst[off - 1, at]
            if self.set is Wide:
                shared_out[at] = total
            else:
                misc_out[...] = total

    STAGES = ("after_pair", "after_far", "after_near", "after_far_b", "after_near_b", "finish")
    units = [Unit(unit) for unit in range(UNITS + 1)]

    def run(stage, *which):
        for unit in which:
            getattr(units[unit], STAGES[stage])()

    def weight_grad(unit, left, right):
        value = right()

        def body(tile):
            rows = pl.ds(pl.multiple_of(tile * 256, 256), 256)
            grads[unit, tile] = dot(left[rows, :], value).astype(LOW).reshape(4, 2, 32, WIDE)

        loop(4, body)
        units[unit].begin()

    def slab_value(index):
        return lambda: slab(index)[...].reshape(512, WIDE)

    before_unit = None
    for j in range(OWN_EXPERTS):
        for kind, left in ((0, x_t), (3, x_t), (6, g_t)):
            weight_grad(kind + j, left, slab_value(kind + j))
            if before_unit is not None:
                run(0, before_unit)
            before_unit = kind + j
    run(0, before_unit)
    run(1, 0, 3, 6, 1)

    def mix_part(block):
        total = None
        for j in range(OWN_EXPERTS):
            part = dot(slab(6 + j, (128, block))[...].reshape(128, WIDE), wd[j])
            total = part if total is None else total + part
        x_all[block] = total.astype(LOW)

    loop(4, mix_part)
    run(1, 4, 7)

    for off in (1, 2, 3):
        dots_copy(off).wait()
        back_copy(off).wait()

    def mix_copy(off):
        return y_copy(MIX, off, x_all.at[(y_at + off) % 4], mix_in.at[off - 1])

    for off in (2, 1, 3):
        mix_copy(off).start()
    taken = dots_send[y_at]
    moe_grad = own_row[...]
    for off in (1, 2, 3):
        taken = taken + dots_in[off - 1]
        moe_grad = moe_grad + row_in[off - 1].astype(F32)
    taken = jnp.concatenate([taken, jnp.zeros((112, 128), F32)], axis=0).T
    own_probs = probs[y_at]
    select = own_probs * (taken - jnp.sum(own_probs * taken, axis=1, keepdims=True))
    select = select.astype(LOW)
    moe_grad = moe_grad + dot_nt(select, router[...])
    router_grad = dot(x_t[:, lane_block(y_at)], select)
    normal = middle[...]
    ffn_r = lax.rsqrt(jnp.mean(normal * normal, axis=1, keepdims=True) + EPS)
    scaled = moe_grad * ffn_gain[...]
    ffn_gain_grad = jnp.sum(moe_grad * normal * ffn_r, axis=0, keepdims=True)
    shrink = ffn_r * ffn_r * ffn_r * jnp.mean(scaled * normal, axis=1, keepdims=True)
    cot[...] = cot[...] + ffn_r * scaled - normal * shrink
    attn_grad = cot[...].astype(LOW)
    for part in (0, 1):
        loads[("bwd", 4 + part)].wait()
    head_grad = dot_nt(attn_grad[:, 0:WIDE], square(weights, 3)) + dot_nt(attn_grad[:, WIDE:], square(weights, 4))
    head_low = head_grad.astype(LOW).astype(F32)
    for c in range(4):
        q_four[4 + c] = four_heads(head_low[:, c * 256 : c * 256 + 128], head_low[:, c * 256 + 128 : c * 256 + 256])
    x_t[:, 0:128] = attn_grad.T

    key_sums, value_sums = pair_in.at[0], pair_in.at[3]

    def attend_back(c):
        heads = q_four[4 + c]
        low = prob_ref(c)[...].reshape(512, 512)
        soft = low.astype(F32)
        weighted = soft * dot_nt(value_block(c), heads)
        sums = jnp.sum(weighted, axis=0, keepdims=True)
        score_grad = ((weighted - soft * sums) * 0.125).astype(LOW)
        value_sums[:, :, :, lane_block(c)] = dot(low, heads).astype(LOW).reshape(4, 4, 32, 128)
        key_sums[:, :, :, lane_block(c)] = dot(score_grad, q_four[c]).astype(LOW).reshape(4, 4, 32, 128)
        first, second = unfold_heads(dot_tn(key_block(c), score_grad))
        q_low[:, lane_block(2 * c)] = turn(first, cosine[...], sine[...], -1.0).astype(LOW)
        q_low[:, lane_block(2 * c + 1)] = turn(second, cosine[...], sine[...], -1.0).astype(LOW)

    loop(4, attend_back)

    def kvg_copies(off):
        to = (y_at + off) % 4
        return [
            pltpu.make_async_remote_copy(
                src_ref=src.at[to], dst_ref=kvg_in.at[off - 1, kind], send_sem=y_send.at[KVG + kind, off - 1],
                recv_sem=y_recv.at[KVG + kind, off - 1], device_id=across(off), device_id_type=MESH,
            )
            for kind, src in ((0, key_sums), (1, value_sums))
        ]

    for off in (2, 1, 3):
        start(kvg_copies(off))

    run(1, 2, 5, 8)
    run(2, 0, 3, 6)
    for part in (0, 1):
        weight_grad(OUT_UNIT + part, x_t.at[:, pl.ds(0, 128)], lambda: joined[:, half[part]])
    run(2, 1, 4)
    for part in (0, 1):
        weight_grad(QUERY_UNIT + part, normed_t, lambda: q_low[:, half[part]])
    run(0, OUT_UNIT, OUT_UNIT + 1, QUERY_UNIT, QUERY_UNIT + 1)
    run(2, 7, 2, 5, 8)
    for part in (0, 1, 2, 3):
        loads[("bwd", part)].wait()
    normed_grad = dot_nt(q_low[:, 0:WIDE], square(weights, 0)) + dot_nt(q_low[:, WIDE:], square(weights, 1))
    input_grad[...] = normed_grad
    for off in (1, 2, 3):
        mix_copy(off).wait()
    total = middle[...] + x_all[y_at].astype(F32)
    for off in (1, 2, 3):
        total = total + mix_in[off - 1].astype(F32)
    hidden_out[...] = total
    run(1, OUT_UNIT, OUT_UNIT + 1)
    run(3, 0, 3, 6, 1, 4)

    for off in (1, 2, 3):
        wait(kvg_copies(off))
    key_back, value_back = key_sums[y_at].reshape(128, WIDE).astype(F32), value_sums[y_at].reshape(128, WIDE).astype(F32)
    for off in (1, 2, 3):
        key_back = key_back + kvg_in[off - 1, 0].reshape(128, WIDE).astype(F32)
        value_back = value_back + kvg_in[off - 1, 1].reshape(128, WIDE).astype(F32)
    q_low[:, half[0]] = turn(key_back, cosine[...], sine[...], -1.0).astype(LOW)
    q_low[:, half[1]] = value_back.astype(LOW)
    weight_grad(KEY_UNIT, normed_t, lambda: q_low[:, half[0]])
    weight_grad(VALUE_UNIT, normed_t, lambda: q_low[:, half[1]])
    normed_grad = input_grad[...] + dot_nt(q_low[:, 0:WIDE], square(weights, 2))
    normed_grad = normed_grad + dot_nt(q_low[:, WIDE:], square(weights, 5))
    hidden = tokens[...].astype(F32)
    attn_r = lax.rsqrt(jnp.mean(hidden * hidden, axis=1, keepdims=True) + EPS)
    scaled = normed_grad * attn_gain[...]
    attn_gain_grad = jnp.sum(normed_grad * hidden * attn_r, axis=0, keepdims=True)
    shrink = attn_r * attn_r * attn_r * jnp.mean(scaled * hidden, axis=1, keepdims=True)
    input_grad[...] = cot[...] + attn_r * scaled - hidden * shrink
    wide_lane = lanes_of((1024, 128))
    gains = jnp.where(
        wide_lane == EXPERTS,
        jnp.broadcast_to(attn_gain_grad, (128, 1024)).T,
        jnp.broadcast_to(ffn_gain_grad, (128, 1024)).T,
    )
    misc[0] = jnp.where(wide_lane < EXPERTS, router_grad, gains).astype(LOW).reshape(4, 4, 2, 32, 128)
    units[UNITS].begin()

    rest = (OUT_UNIT, OUT_UNIT + 1, QUERY_UNIT, QUERY_UNIT + 1, KEY_UNIT, VALUE_UNIT, UNITS)
    run(0, KEY_UNIT, VALUE_UNIT, UNITS)
    run(1, QUERY_UNIT, QUERY_UNIT + 1)
    run(2, OUT_UNIT, OUT_UNIT + 1)
    run(1, KEY_UNIT, VALUE_UNIT, UNITS)
    run(3, 7, 2, 5, 8)
    run(4, 0, 3, 6, 1, 4, 7, 2, 5, 8)
    run(3, OUT_UNIT, OUT_UNIT + 1)
    run(2, QUERY_UNIT, QUERY_UNIT + 1, KEY_UNIT, VALUE_UNIT, UNITS)
    run(4, OUT_UNIT, OUT_UNIT + 1)
    run(3, QUERY_UNIT, QUERY_UNIT + 1, KEY_UNIT, VALUE_UNIT, UNITS)
    run(4, QUERY_UNIT, QUERY_UNIT + 1, KEY_UNIT, VALUE_UNIT, UNITS)
    run(5, *rest)


def layer(*args):
    vmem = pl.BlockSpec(memory_space=pltpu.VMEM)
    smem = pl.BlockSpec(memory_space=pltpu.SMEM)
    far = pl.BlockSpec(memory_space=pl.ANY)
    low = lambda *shape: pltpu.VMEM(shape, LOW)
    wide = lambda *shape: pltpu.VMEM(shape, F32)
    sems = pltpu.SemaphoreType.DMA
    scratch = [
        low(UNITS + 1, *BIG), low(6, *BIG), low(3, 512, 1024), low(1024, 128), wide(128, 1024), wide(128, 128), wide(128, 128),
        low(128, 1024), low(1024, 128), low(128, 1024), low(128, 1024), low(8, 512, 128),
        low(4, 128, 1024), low(4, 128, 1024), low(4, 128, 1024), low(4, 128, 128),
        low(1024, 512), low(1024, 512), wide(4, 128, 128), wide(512, 128), wide(512, 128),
        wide(4, 16, 128), wide(3, 16, 128), low(4, 128, 1024), low(3, 128, 1024),
        low(3, 128, 1024), low(3, 2, 4, 32, WIDE),
    ]
    for count, width in ((UNITS, WIDE), (1, 128)):
        if count == 1:
            scratch += [low(1, 4, 4, 2, 32, width)]
        scratch += [low(count, 4, 4, 32, width), low(count, 2, 32, width), low(count, 2, 32, width)]
        scratch += [low(count, 4, 32, width), low(count, 4, 32, width)]
        scratch += [low(count, 16, width), low(count, 16, width), low(count, 32, width), low(count, 32, width)]
        shared = count - EXPERT_UNITS if count == UNITS else 1
        scratch += [wide(shared, 32, width), wide(3, shared, 8, width)]
    scratch += [sems((9, 3)), sems((9, 3)), sems((12, UNITS + 1)), sems((12, UNITS + 1)), sems((20,))]
    shape = jax.ShapeDtypeStruct
    return pl.pallas_call(
        layer_kernel,
        out_shape=(
            shape((128, 1024), F32),
            shape((128, 1024), F32),
            shape((EXPERT_UNITS, 32, WIDE), F32),
            shape((UNITS - EXPERT_UNITS, 8, WIDE), F32),
            shape((8, 128), F32),
        ),
        in_specs=[vmem, vmem, vmem, smem, vmem, vmem, vmem] + [far] * 10,
        out_specs=(vmem,) * 5,
        scratch_shapes=scratch,
        compiler_params=pltpu.CompilerParams(
            collective_id=0, has_side_effects=True, vmem_limit_bytes=60 * 2**20
        ),
        name="layer",
    )(*args)


def rope_tables(length):
    inverse = np.float32(10000.0) ** (-np.arange(32, dtype=np.float32) / np.float32(32))
    angles = np.arange(length, dtype=np.float32)[:, None] * inverse[None, :]
    cosine, sine = np.cos(angles), np.sin(angles)
    return np.tile(cosine, (1, 4)), np.concatenate([-sine, sine, -sine, sine], axis=1)


def per_device(
    tokens, routes, slot_order, prefix, attn_gain, w_query, w_key, w_value, w_out, ffn_gain, w_router,
    w_gate, w_up, w_down, cotangent,
):
    cosine, sine = rope_tables(512)
    hidden_out, input_grad, expert_done, shared, misc = layer(
        tokens, routes[0], slot_order[0], prefix, attn_gain, ffn_gain, w_router[0],
        w_query.reshape(4, 4, 2, 32, 1024), w_key.reshape(BIG), w_value.reshape(BIG), w_out.reshape(4, 4, 2, 32, 1024),
        w_gate.reshape(3, *BIG), w_up.reshape(3, *BIG), w_down[0], cotangent, jnp.asarray(cosine), jnp.asarray(sine),
    )
    at = lambda unit: unit - EXPERT_UNITS
    return (
        hidden_out,
        input_grad,
        misc[:, EXPERTS][None],
        jnp.concatenate([shared[at(QUERY_UNIT)], shared[at(QUERY_UNIT + 1)]], axis=1)[None],
        shared[at(KEY_UNIT)][None],
        shared[at(VALUE_UNIT)][None],
        jnp.concatenate([shared[at(OUT_UNIT)], shared[at(OUT_UNIT + 1)]], axis=1).T[None],
        misc[:, EXPERTS + 1][None],
        misc[:, :EXPERTS][None],
        expert_done[0:3][None],
        expert_done[3:6][None],
        expert_done[6:9].transpose(0, 2, 1)[None],
    )


def solution(mesh):
    both = ("group", "expert")
    in_specs = (
        P(both, None), P(None, both, None), P(None, both, None), P("group"), P(), P(), P(), P(), P(), P(), P(),
        P(None, "expert", None, None), P(None, "expert", None, None), P(None, "expert", None, None), P(both, None),
    )
    out_specs = (
        P(both, None), P(both, None), P(None, both), P(None, both, None), P(None, both, None), P(None, both, None),
        P(None, None, both), P(None, both), P(None, both, None), P(None, "expert", "group", None),
        P(None, "expert", "group", None), P(None, "expert", None, "group"),
    )
    return jax.shard_map(per_device, mesh=mesh, in_specs=in_specs, out_specs=out_specs, check_vma=False)
```

profile of v0, /device:TPU:0, one launch (start us, length us, event | category | flops | bytes accessed | tf_op | source)
XLA Modules:
  0.0 154.3 jit_solution(17507396733565297683)
XLA Ops:
  0.6 1.6 %copy.32 = bf16[1,1024,12]{2,1,0:T(8,128)(2,1)} copy(bf16[1,1024,12]{1,2,0:T(8,128)(2,1)} %param.27) | data formatting | bytes 49152 | tf_op args[10]
  2.3 1.4 copy.31
  4.3 139.4 %layer.1 = (f32[128,1024]{1,0:T(8,128)}, f32[128,1024]{1,0:T(8,128)}, f32[9,32,512]{2,1,0:T(8,128)}, f32[6,8,512]{2,1,0:T(8,128)}, f32[8,128]{1,0:T(8,128)}) custom-call(bf16[128,1024]{1,0:T(8,128)(2,1)} %tokens.1, s32[128,8]{1,0:T(8,128)} %bitcast.44, s32[1,128]{1,0:T(1,128)} %bitcast.45, s32[1]{0:T(128)S(6)} %copy.35.prefix, f32[1,1024]{1,0:T(1,128)} %attn_gain.1, ...), custom_call_target="tpu_custom_call" | custom-call | tf_op jit(solution)/shard_map/layer/pallas_call | solution.py:647
  143.8 1.4 slice_bitcast_fusion.4
  145.2 0.6 maximum_bitcast_fusion
  145.8 1.9 %slice_bitcast_fusion = (f32[1,3,512,32]{2,3,1,0:T(8,128)}, f32[1,3,32,512]{3,2,1,0:T(8,128)}, f32[1,3,32,512]{3,2,1,0:T(8,128)}) fusion(f32[9,32,512]{2,1,0:T(8,128)} %get-tuple-element.21), kind=kLoop, calls=%fused_computation | loop fusion | bytes 1179648 | tf_op jit(solution)/shard_map/broadcast_in_dim | solution.py:696
  147.7 1.5 slice_reduce_fusion
  149.2 1.3 slice_bitcast_fusion.7
  150.5 1.9 %copy.36 = f32[128,1024]{1,0:T(8,128)} copy(f32[128,1024]{1,0:T(8,128)} %get-tuple-element.47) | data formatting | bytes 1048576
  152.4 1.9 %copy.37 = f32[128,1024]{1,0:T(8,128)} copy(f32[128,1024]{1,0:T(8,128)} %get-tuple-element.48) | data formatting | bytes 1048576
where the time goes:
time: 155 us; the launch traced here: 154 us
  Pallas kernels  139 us (90%)
  local copies, waits for them, and re-layouts  12.9 us (8%)
    pallas_call x1, Pallas kernels, layer(): pl.pallas_call(layer_kernel, out_shape=(shape((128, 1024), F32), shape((1...  139 us
    unnamed x4, local copies, waits for them, and re-layouts  6.81 us

commit v1 on v0

--- a/solution.py
+++ b/solution.py
@@ -18,7 +18,6 @@
 WIDE = 512
 KEY_UNIT, VALUE_UNIT, QUERY_UNIT, OUT_UNIT, SPARE = 9, 10, 11, 13, 15
 BIG = (4, 4, 2, 32, WIDE)
-KV, COT, CODE, ROWS, BACK, DOTS, MIX, KVG = range(8)
 
 
 def group_of(x_at, z_at, core):
@@ -46,7 +45,7 @@
 
 
 def turn(values, cosine, sine, sign):
-    first = lanes_of((128, 128)) % 64 < 32
+    first = lanes_of((values.shape[0], 128)) % 64 < 32
     parts = []
     for at in range(values.shape[1] // 128):
         part = values[:, at * 128 : at * 128 + 128]
@@ -92,18 +91,19 @@
     wq_far, wk_far, wv_far, wo_far, wg_far, wu_far, wd_far, cot_far, cos_far, sin_far,
     hidden_out, input_grad, expert_out, shared_out, misc_out,
     grads, weights, wd, router, cot, cosine, sine,
-    normed, normed_t, q_low, joined, q_four, kv_all, x_all, g_all, code_all,
+    normed_all, joined, q_four, kv_all, x_all, g_all, code_all,
     x_t, g_t, probs, gates, own_dots, dots_send, dots_in, row_send, row_in, mix_in, kvg_in,
     pair_in, lo_in, hi_in, minus_in, plus_in, lo_in_b, hi_in_b, minus_in_b, plus_in_b, last, last_in,
     misc, misc_pair, misc_lo, misc_hi, misc_minus, misc_plus, misc_lo_b, misc_hi_b, misc_minus_b, misc_plus_b,
     misc_last, misc_last_in,
     y_send, y_recv, send_sem, recv_sem, local_sem,
 ):
-    middle, own_row = hidden_out, input_grad
     group = lax.axis_index("group")
     y_at = lax.axis_index("expert")
     x_at, z_at, core = group // 8, (group // 2) % 4, group % 2
     spots = (x_at, z_at)
+    own_rows = pl.ds(pl.multiple_of(y_at * 128, 128), 128)
+    middle, own_row, q_low, normed_t = hidden_out, input_grad, normed_all.at[y_at], g_t
 
     def device(axis, offset):
         if axis == 0:
@@ -128,22 +128,18 @@
         loads[name] = copy
         copy.start()
 
-    def attn_loads(tag, ref, order_of):
-        wk_to, wv_to, wq_to, wo_to = order_of
+    def load_keys(tag, ref, wk_to, wv_to):
         load((tag, 0), wk_far, ref.at[wk_to])
         load((tag, 1), wv_far, ref.at[wv_to])
+
+    def load_pair(tag, at, src, ref, to):
         for part in (0, 1):
-            load((tag, 2 + part), wq_far.at[:, :, :, :, half[part]], ref.at[wq_to + part])
-        for part in (0, 1):
-            load((tag, 4 + part), wo_far.at[:, :, :, :, half[part]], ref.at[wo_to + part])
-
-    load("cos", cos_far.at[pl.ds(y_at * 128, 128)], cosine)
-    load("sin", sin_far.at[pl.ds(y_at * 128, 128)], sine)
-    attn_loads("fwd", grads, (0, 1, 2, 4))
-    load("cot", cot_far, cot)
-    load("wg", wg_far, weights.at[pl.ds(0, 3)])
-    load("wu", wu_far, weights.at[pl.ds(3, 3)])
-    load("wd", wd_far, wd)
+            load((tag, at + part), src.at[:, :, :, :, half[part]], ref.at[to + part])
+
+    load_pair("fwd", 2, wq_far, grads, 2)
+    load("cos", cos_far, cosine)
+    load("sin", sin_far, sine)
+    load_keys("fwd", grads, 0, 1)
 
     def square(ref, unit):
         return ref[unit].reshape(1024, WIDE)
@@ -159,21 +155,18 @@
 
     hidden = tokens[...].astype(F32)
     attn_r = lax.rsqrt(jnp.mean(hidden * hidden, axis=1, keepdims=True) + EPS)
-    normed[...] = (hidden * attn_r * attn_gain[...]).astype(LOW)
-    for name in ("cos", "sin", ("fwd", 0), ("fwd", 1)):
-        loads[name].wait()
-    kv_all[y_at, :, 0:WIDE] = turn(dot(normed[...], square(grads, 0)), cosine[...], sine[...], 1.0).astype(LOW)
-    kv_all[y_at, :, WIDE:] = dot(normed[...], square(grads, 1)).astype(LOW)
+    normed_all[y_at] = (hidden * attn_r * attn_gain[...]).astype(LOW)
     pl.semaphore_wait(barrier, len(peers))
 
-    def y_copy(kind, off, src, dst):
+    y_used = []
+
+    def y_copy(off, src, dst):
+        at = len(y_used)
+        y_used.append(off)
         return pltpu.make_async_remote_copy(
-            src_ref=src, dst_ref=dst, send_sem=y_send.at[kind, off - 1], recv_sem=y_recv.at[kind, off - 1],
+            src_ref=src, dst_ref=dst, send_sem=y_send.at[at], recv_sem=y_recv.at[at],
             device_id=across(off), device_id_type=MESH,
         )
-
-    def share(kind, ref):
-        return [y_copy(kind, off, ref.at[y_at], ref.at[y_at]) for off in (2, 1, 3)]
 
     def start(copies):
         for copy in copies:
@@ -183,22 +176,80 @@
         for copy in copies:
             copy.wait()
 
-    kv_share = share(KV, kv_all)
-    start(kv_share)
-
+    left, right = (y_at + 3) % 4, (y_at + 1) % 4
+    low_rows, high_rows = pl.ds(0, 64), pl.ds(64, 64)
+
+    class Gather:
+        def __init__(self, ref):
+            def pass_on(block, rows, off):
+                return y_copy(off, ref.at[block, rows], ref.at[block, rows])
+
+            self.first = [pass_on(y_at, low_rows, 1), pass_on(y_at, high_rows, 3)]
+            self.first += [pass_on(y_at, high_rows, 1), pass_on(y_at, low_rows, 3)]
+            self.second = [pass_on(left, low_rows, 1), pass_on(right, high_rows, 3)]
+
+        def start(self):
+            start(self.first)
+
+        def forward(self):
+            for came, on in zip(self.first, self.second):
+                came.wait_recv()
+                on.start()
+
+        def finish(self):
+            for copy in self.first[2:]:
+                copy.wait_recv()
+            for copy in self.first:
+                copy.wait_send()
+            wait(self.second)
+
+    class Scatter:
+        def __init__(self, block, land):
+            self.block, self.land = block, land
+            far = (y_at + 2) % 4
+            self.far = [y_copy(1, block(far, 0), land(0, 0)), y_copy(3, block(far, 1), land(0, 1))]
+            self.near = [y_copy(1, block(right, 1), land(1, 1)), y_copy(3, block(left, 0), land(2, 0))]
+            self.last = [y_copy(1, block(right, 0), land(1, 0)), y_copy(3, block(left, 1), land(2, 1))]
+
+        def start(self):
+            start(self.far)
+            start(self.near)
+
+        def turn(self):
+            for part, to in ((0, right), (1, left)):
+                self.far[part].wait()
+                ref = self.block(to, part)
+                ref[...] = sum32(ref[...], self.land(0, part)[...])
+                self.last[part].start()
+
+        def finish(self):
+            wait(self.near)
+            wait(self.last)
+
+    normed_share = Gather(normed_all)
+    normed_share.start()
+    load_pair("fwd", 4, wo_far, grads, 4)
+    load("cot", cot_far, cot)
+    load("wg", wg_far, weights.at[pl.ds(0, 3)])
+    load("wu", wu_far, weights.at[pl.ds(3, 3)])
+    load("wd", wd_far, wd)
+
+    for name in ("cos", "sin"):
+        loads[name].wait()
     for part in (0, 1):
         loads[("fwd", 2 + part)].wait()
-        turned = turn(dot(normed[...], square(grads, 2 + part)), cosine[...], sine[...], 1.0)
+        turned = turn(dot(normed_all[y_at], square(grads, 2 + part)), cosine[own_rows, :], sine[own_rows, :], 1.0)
         turned = turned.astype(LOW).astype(F32)
         for c in (0, 1):
             q_four[part * 2 + c] = four_heads(
                 turned[:, c * 256 : c * 256 + 128], turned[:, c * 256 + 128 : c * 256 + 256]
             )
 
-    lane = lanes_of((128, 128))
+    expert_at = lax.broadcasted_iota(jnp.int32, (128, 128), 0)
     member = jnp.zeros((128, 128), F32)
-    for pick in range(routes.shape[1]):
-        member = member + jnp.where(routes[:, pick : pick + 1] == lane, 1.0, 0.0)
+    for pick in range(routes.shape[0]):
+        member = member + jnp.where(routes[pick : pick + 1, :] == expert_at, 1.0, 0.0)
+    member = member.T
     ranks = jnp.broadcast_to(order[...].astype(F32), (128, 128))
     earlier = jnp.where(ranks < ranks.T, 1.0, 0.0).astype(LOW)
     before = dot(earlier, member.astype(LOW))
@@ -206,14 +257,25 @@
     loads["cot"].wait()
     g_all[y_at] = cot[...].astype(LOW)
     router[...] = jnp.zeros_like(router)
-    router[:, 0:EXPERTS] = w_router[...]
-    normed_t[...] = normed[...].T
-
-    wait(kv_share)
-    code_share = share(CODE, code_all)
-    g_share = share(COT, g_all)
+    router[0:EXPERTS, :] = w_router[...]
+    for part in (0, 1):
+        loads[("fwd", part)].wait()
+    normed_share.forward()
+    normed_share.finish()
+
+    def keys_values(part):
+        lanes = lane_block(part, 256)
+        inputs = normed_all[...].reshape(512, 1024)
+        keys = turn(dot(inputs, grads[0, :, :, :, :, lanes].reshape(1024, 256)), cosine[...], sine[...], 1.0)
+        kv_all[:, :, lanes] = keys.astype(LOW).reshape(4, 128, 256)
+        values = dot(inputs, grads[1, :, :, :, :, lanes].reshape(1024, 256))
+        kv_all[:, :, lane_block(2 + part, 256)] = values.astype(LOW).reshape(4, 128, 256)
+
+    loop(2, keys_values)
+    g_share = Gather(g_all)
+    g_share.start()
+    code_share = [y_copy(off, code_all.at[y_at], code_all.at[y_at]) for off in (1, 3, 2)]
     start(code_share)
-    start(g_share)
 
     def visible():
         shape = (512, 512)
@@ -246,11 +308,10 @@
         middle[:, half[part]] = tokens[:, half[part]].astype(F32) + dot(joined[...], square(grads, 4 + part))
     ffn_r = lax.rsqrt(jnp.mean(middle[...] * middle[...], axis=1, keepdims=True) + EPS)
     x_all[y_at] = (middle[...] * ffn_r * ffn_gain[...]).astype(LOW)
-    x_share = share(ROWS, x_all)
-    start(x_share)
+    x_share = Gather(x_all)
+    x_share.start()
 
     wait(code_share)
-    wait(g_share)
 
     def stand(ref, out):
         def body(block):
@@ -258,13 +319,13 @@
 
         loop(4, body)
 
-    stand(g_all, g_t)
-    wait(x_share)
-    stand(x_all, x_t)
+    x_share.forward()
+    x_share.finish()
+    g_share.forward()
 
     code = code_all[...].reshape(512, 128).astype(F32)
     in_use = code > 0.5
-    logits = jnp.where(in_use, dot(x_all[...].reshape(512, 1024), router[...]), -1e30)
+    logits = jnp.where(in_use, dot_nt(x_all[...].reshape(512, 1024), router[...]), -1e30)
     raised = jnp.where(in_use, jnp.exp(logits - jnp.max(logits, axis=1, keepdims=True)), 0.0)
     soft = raised / jnp.sum(raised, axis=1, keepdims=True)
     probs[...] = soft.reshape(4, 128, 128)
@@ -272,55 +333,74 @@
     own_dots[...] = jnp.zeros_like(own_dots)
     for name in ("wg", "wu", "wd"):
         loads[name].wait()
-
-    def expert_step(step):
-        j, part = step // 2, step % 2
-        rows = pl.ds(pl.multiple_of(part * 256, 256), 256)
-        blocks = pl.ds(part * 2, 2)
-        here = lanes_of((256, 128)) == y_at * OWN_EXPERTS + j
-        gate_of = jnp.sum(jnp.where(here, gates[rows, :], 0.0), axis=1, keepdims=True)
-        inputs = x_all[blocks].reshape(256, 1024)
-        gate_lin = dot(inputs, square(weights, j))
-        up_lin = dot(inputs, square(weights, 3 + j))
-        outer = dot_nt(g_all[blocks].reshape(256, 1024), wd[j])
+    slab_shape = (2, 4, 2, 32, 256)
+
+    def gate_of(j):
+        here = lanes_of((512, 128)) == y_at * OWN_EXPERTS + j
+        return here, jnp.sum(jnp.where(here, gates[...], 0.0), axis=1, keepdims=True)
+
+    def expert_forward(step):
+        j, lanes = step // 2, lane_block(step % 2, 256)
+        inputs = x_all[...].reshape(512, 1024)
+        gate_lin = dot(inputs, weights[j, :, :, :, :, lanes].reshape(1024, 256))
+        up_lin = dot(inputs, weights[3 + j, :, :, :, :, lanes].reshape(1024, 256))
         sig = 1.0 / (1.0 + jnp.exp(-gate_lin))
         silu = gate_lin * sig
-        act = (silu * up_lin).astype(LOW).astype(F32)
-        taken = jnp.where(gate_of > 0.0, jnp.sum(act * outer, axis=1, keepdims=True), 0.0)
-        own_dots[rows, :] = jnp.where(here, taken, own_dots[rows, :])
-        outer = outer * gate_of
-        shape = (4, 2, 32, WIDE)
-        slab(6 + j, (256, part))[...] = (act * gate_of).astype(LOW).reshape(shape)
-        slab(j, (256, part))[...] = (outer * up_lin * sig * (1.0 + gate_lin * (1.0 - sig))).astype(LOW).reshape(shape)
-        slab(3 + j, (256, part))[...] = (outer * silu).astype(LOW).reshape(shape)
-
-    loop(6, expert_step)
-
-    def dots_copy(off):
-        return y_copy(DOTS, off, dots_send.at[(y_at + off) % 4], dots_in.at[off - 1])
-
-    def back_copy(off):
-        return y_copy(BACK, off, row_send.at[(y_at + off) % 4], row_in.at[off - 1])
-
+        act = (silu * up_lin).astype(LOW).astype(F32) * gate_of(j)[1]
+        slab(6 + j)[:, :, :, :, lanes] = act.astype(LOW).reshape(slab_shape)
+        slab(j)[:, :, :, :, lanes] = (up_lin * sig * (1.0 + gate_lin * (1.0 - sig))).astype(LOW).reshape(slab_shape)
+        slab(3 + j)[:, :, :, :, lanes] = silu.astype(LOW).reshape(slab_shape)
+
+    def expert_back(step):
+        j, lanes = step // 2, lane_block(step % 2, 256)
+        here, gate = gate_of(j)
+        outer = dot_nt(g_all[...].reshape(512, 1024), wd[j, lanes, :])
+        act = slab(6 + j)[:, :, :, :, lanes].reshape(512, 256).astype(F32)
+        own_dots[...] += jnp.where(here, jnp.sum(act * outer, axis=1, keepdims=True), 0.0)
+        outer = outer * gate
+        for index in (j, 3 + j):
+            slope = slab(index)[:, :, :, :, lanes].reshape(512, 256).astype(F32)
+            slab(index)[:, :, :, :, lanes] = (outer * slope).astype(LOW).reshape(slab_shape)
+
+    loop(2 * OWN_EXPERTS, expert_forward)
+    g_share.finish()
+    loop(2 * OWN_EXPERTS, expert_back)
+
+    dots_copies = [y_copy(off, dots_send.at[(y_at + off) % 4], dots_in.at[off - 1]) for off in (1, 3, 2)]
     for block in range(4):
         dots_send[block] = own_dots[block * 128 : block * 128 + 128, :].T[0:16, :]
-    for off in (2, 1, 3):
-        dots_copy(off).start()
-
-    def row_part(block):
+    start(dots_copies)
+
+    def row_part(first, second):
         total = None
         for j in range(OWN_EXPERTS):
             for kind in (0, 3):
-                lin = slab(kind + j, (128, block))[...].reshape(128, WIDE)
-                part = dot_nt(lin, square(weights, kind + j))
+                pair = [slab(kind + j, (128, block))[...].reshape(128, WIDE) for block in (first, second)]
+                part = dot_nt(jnp.concatenate(pair, axis=0), square(weights, kind + j))
                 total = part if total is None else total + part
         return total
 
-    for off in (2, 1, 3):
-        row_send[(y_at + off) % 4] = row_part((y_at + off) % 4).astype(LOW)
-        back_copy(off).start()
-    own_row[...] = row_part(y_at)
-    attn_loads("bwd", weights, (2, 5, 0, 3))
+    def across_block(off):
+        return (y_at + off) % 4
+
+    rows = row_part(across_block(2), across_block(1))
+    for off in (2, 1):
+        row_send[across_block(off)] = rows[128 * (2 - off) : 128 * (3 - off)].astype(LOW)
+    rows_back = Scatter(
+        lambda block, part: row_send.at[block, pl.ds(64 * part, 64)], lambda at, part: row_in.at[at, pl.ds(64 * part, 64)]
+    )
+    start(rows_back.far)
+    rows_back.near[0].start()
+    rows = row_part(across_block(3), y_at)
+    row_send[across_block(3)] = rows[0:128].astype(LOW)
+    rows_back.near[1].start()
+    own_row[...] = rows[128:256]
+    stand(x_all, x_t)
+    stand(g_all, g_t)
+    rows_back.turn()
+    load_pair("bwd", 4, wo_far, weights, 3)
+    load_pair("bwd", 2, wq_far, weights, 0)
+    load_keys("bwd", weights, 2, 5)
 
     class Wide:
         src, pair, lo, hi, minus, plus = grads, pair_in, lo_in, hi_in, minus_in, plus_in
@@ -458,13 +538,7 @@
             getattr(units[unit], STAGES[stage])()
 
     def weight_grad(unit, left, right):
-        value = right()
-
-        def body(tile):
-            rows = pl.ds(pl.multiple_of(tile * 256, 256), 256)
-            grads[unit, tile] = dot(left[rows, :], value).astype(LOW).reshape(4, 2, 32, WIDE)
-
-        loop(4, body)
+        grads[unit] = dot(left[...], right()).astype(LOW).reshape(BIG)
         units[unit].begin()
 
     def slab_value(index):
@@ -472,43 +546,46 @@
 
     before_unit = None
     for j in range(OWN_EXPERTS):
-        for kind, left in ((0, x_t), (3, x_t), (6, g_t)):
-            weight_grad(kind + j, left, slab_value(kind + j))
+        for kind, turned_rows in ((0, x_t), (3, x_t), (6, g_t)):
+            weight_grad(kind + j, turned_rows, slab_value(kind + j))
             if before_unit is not None:
                 run(0, before_unit)
             before_unit = kind + j
     run(0, before_unit)
     run(1, 0, 3, 6, 1)
 
-    def mix_part(block):
+    def mix_part(part):
         total = None
         for j in range(OWN_EXPERTS):
-            part = dot(slab(6 + j, (128, block))[...].reshape(128, WIDE), wd[j])
-            total = part if total is None else total + part
-        x_all[block] = total.astype(LOW)
-
-    loop(4, mix_part)
+            piece = dot(slab(6 + j, (256, part))[...].reshape(256, WIDE), wd[j])
+            total = piece if total is None else total + piece
+        x_all[pl.ds(part * 2, 2)] = total.astype(LOW).reshape(2, 128, 1024)
+
+    loop(2, mix_part)
     run(1, 4, 7)
 
-    for off in (1, 2, 3):
-        dots_copy(off).wait()
-        back_copy(off).wait()
-
-    def mix_copy(off):
-        return y_copy(MIX, off, x_all.at[(y_at + off) % 4], mix_in.at[off - 1])
-
-    for off in (2, 1, 3):
-        mix_copy(off).start()
+    def normed_stand(block):
+        normed_t[:, lane_block(block)] = normed_all[block].T
+
+    loop(4, normed_stand)
+
+    wait(dots_copies)
+    rows_back.finish()
+    mix_back = Scatter(
+        lambda block, part: x_all.at[block, pl.ds(64 * part, 64)], lambda at, part: mix_in.at[at, pl.ds(64 * part, 64)]
+    )
+    mix_back.start()
     taken = dots_send[y_at]
     moe_grad = own_row[...]
     for off in (1, 2, 3):
         taken = taken + dots_in[off - 1]
-        moe_grad = moe_grad + row_in[off - 1].astype(F32)
+    for at in (1, 2):
+        moe_grad = moe_grad + row_in[at].astype(F32)
     taken = jnp.concatenate([taken, jnp.zeros((112, 128), F32)], axis=0).T
     own_probs = probs[y_at]
-    select = own_probs * (taken - jnp.sum(own_probs * taken, axis=1, keepdims=True))
+    select = taken - own_probs * jnp.sum(taken, axis=1, keepdims=True)
     select = select.astype(LOW)
-    moe_grad = moe_grad + dot_nt(select, router[...])
+    moe_grad = moe_grad + dot(select, router[...])
     router_grad = dot(x_t[:, lane_block(y_at)], select)
     normal = middle[...]
     ffn_r = lax.rsqrt(jnp.mean(normal * normal, axis=1, keepdims=True) + EPS)
@@ -521,72 +598,73 @@
         loads[("bwd", 4 + part)].wait()
     head_grad = dot_nt(attn_grad[:, 0:WIDE], square(weights, 3)) + dot_nt(attn_grad[:, WIDE:], square(weights, 4))
     head_low = head_grad.astype(LOW).astype(F32)
+
+    def head_ref(c):
+        return x_t.at[lane_block(c % 2, 512), lane_block(1 + c // 2)]
+
     for c in range(4):
-        q_four[4 + c] = four_heads(head_low[:, c * 256 : c * 256 + 128], head_low[:, c * 256 + 128 : c * 256 + 256])
+        head_ref(c)[...] = four_heads(head_low[:, c * 256 : c * 256 + 128], head_low[:, c * 256 + 128 : c * 256 + 256])
     x_t[:, 0:128] = attn_grad.T
 
     key_sums, value_sums = pair_in.at[0], pair_in.at[3]
 
     def attend_back(c):
-        heads = q_four[4 + c]
+        heads = head_ref(c)[...]
         low = prob_ref(c)[...].reshape(512, 512)
         soft = low.astype(F32)
         weighted = soft * dot_nt(value_block(c), heads)
         sums = jnp.sum(weighted, axis=0, keepdims=True)
         score_grad = ((weighted - soft * sums) * 0.125).astype(LOW)
         value_sums[:, :, :, lane_block(c)] = dot(low, heads).astype(LOW).reshape(4, 4, 32, 128)
-        key_sums[:, :, :, lane_block(c)] = dot(score_grad, q_four[c]).astype(LOW).reshape(4, 4, 32, 128)
+        key_part = turn(dot(score_grad, q_four[c]), cosine[...], sine[...], -1.0)
+        key_sums[:, :, :, lane_block(c)] = key_part.astype(LOW).reshape(4, 4, 32, 128)
         first, second = unfold_heads(dot_tn(key_block(c), score_grad))
-        q_low[:, lane_block(2 * c)] = turn(first, cosine[...], sine[...], -1.0).astype(LOW)
-        q_low[:, lane_block(2 * c + 1)] = turn(second, cosine[...], sine[...], -1.0).astype(LOW)
+        own_cosine, own_sine = cosine[own_rows, :], sine[own_rows, :]
+        q_low[:, lane_block(2 * c)] = turn(first, own_cosine, own_sine, -1.0).astype(LOW)
+        q_low[:, lane_block(2 * c + 1)] = turn(second, own_cosine, own_sine, -1.0).astype(LOW)
 
     loop(4, attend_back)
-
-    def kvg_copies(off):
-        to = (y_at + off) % 4
-        return [
-            pltpu.make_async_remote_copy(
-                src_ref=src.at[to], dst_ref=kvg_in.at[off - 1, kind], send_sem=y_send.at[KVG + kind, off - 1],
-                recv_sem=y_recv.at[KVG + kind, off - 1], device_id=across(off), device_id_type=MESH,
-            )
-            for kind, src in ((0, key_sums), (1, value_sums))
-        ]
-
-    for off in (2, 1, 3):
-        start(kvg_copies(off))
+    mix_back.turn()
+    kv_back = Scatter(lambda block, part: (key_sums, value_sums)[part].at[block], lambda at, part: kvg_in.at[at, part])
+    kv_back.start()
 
     run(1, 2, 5, 8)
     run(2, 0, 3, 6)
     for part in (0, 1):
         weight_grad(OUT_UNIT + part, x_t.at[:, pl.ds(0, 128)], lambda: joined[:, half[part]])
+    weight_grad(KEY_UNIT, normed_t, lambda: key_sums[...].reshape(512, WIDE))
+    weight_grad(VALUE_UNIT, normed_t, lambda: value_sums[...].reshape(512, WIDE))
+    run(0, OUT_UNIT, OUT_UNIT + 1)
     run(2, 1, 4)
     for part in (0, 1):
-        weight_grad(QUERY_UNIT + part, normed_t, lambda: q_low[:, half[part]])
-    run(0, OUT_UNIT, OUT_UNIT + 1, QUERY_UNIT, QUERY_UNIT + 1)
+        weight_grad(QUERY_UNIT + part, normed_t.at[:, lane_block(y_at)], lambda: q_low[:, half[part]])
+    run(0, KEY_UNIT, VALUE_UNIT)
     run(2, 7, 2, 5, 8)
+    run(1, OUT_UNIT, OUT_UNIT + 1)
+    run(0, QUERY_UNIT, QUERY_UNIT + 1)
     for part in (0, 1, 2, 3):
         loads[("bwd", part)].wait()
     normed_grad = dot_nt(q_low[:, 0:WIDE], square(weights, 0)) + dot_nt(q_low[:, WIDE:], square(weights, 1))
     input_grad[...] = normed_grad
-    for off in (1, 2, 3):
-        mix_copy(off).wait()
+    kv_back.turn()
+    mix_back.finish()
     total = middle[...] + x_all[y_at].astype(F32)
-    for off in (1, 2, 3):
-        total = total + mix_in[off - 1].astype(F32)
+    for at in (1, 2):
+        total = total + mix_in[at].astype(F32)
     hidden_out[...] = total
-    run(1, OUT_UNIT, OUT_UNIT + 1)
     run(3, 0, 3, 6, 1, 4)
-
-    for off in (1, 2, 3):
-        wait(kvg_copies(off))
+    run(1, KEY_UNIT, VALUE_UNIT)
+    run(2, OUT_UNIT, OUT_UNIT + 1)
+    run(1, QUERY_UNIT, QUERY_UNIT + 1)
+    run(4, 0, 3, 6, 1, 4)
+
+    kv_back.finish()
     key_back, value_back = key_sums[y_at].reshape(128, WIDE).astype(F32), value_sums[y_at].reshape(128, WIDE).astype(F32)
-    for off in (1, 2, 3):
-        key_back = key_back + kvg_in[off - 1, 0].reshape(128, WIDE).astype(F32)
-        value_back = value_back + kvg_in[off - 1, 1].reshape(128, WIDE).astype(F32)
-    q_low[:, half[0]] = turn(key_back, cosine[...], sine[...], -1.0).astype(LOW)
+    for at in (1, 2):
+        key_back = key_back + kvg_in[at, 0].reshape(128, WIDE).astype(F32)
+        value_back = value_back + kvg_in[at, 1].reshape(128, WIDE).astype(F32)
+    q_low[:, half[0]] = key_back.astype(LOW)
     q_low[:, half[1]] = value_back.astype(LOW)
-    weight_grad(KEY_UNIT, normed_t, lambda: q_low[:, half[0]])
-    weight_grad(VALUE_UNIT, normed_t, lambda: q_low[:, half[1]])
     normed_grad = input_grad[...] + dot_nt(q_low[:, 0:WIDE], square(weights, 2))
     normed_grad = normed_grad + dot_nt(q_low[:, WIDE:], square(weights, 5))
     hidden = tokens[...].astype(F32)
@@ -605,17 +683,18 @@
     units[UNITS].begin()
 
     rest = (OUT_UNIT, OUT_UNIT + 1, QUERY_UNIT, QUERY_UNIT + 1, KEY_UNIT, VALUE_UNIT, UNITS)
-    run(0, KEY_UNIT, VALUE_UNIT, UNITS)
-    run(1, QUERY_UNIT, QUERY_UNIT + 1)
-    run(2, OUT_UNIT, OUT_UNIT + 1)
-    run(1, KEY_UNIT, VALUE_UNIT, UNITS)
     run(3, 7, 2, 5, 8)
-    run(4, 0, 3, 6, 1, 4, 7, 2, 5, 8)
+    run(2, KEY_UNIT, VALUE_UNIT)
+    run(0, UNITS)
     run(3, OUT_UNIT, OUT_UNIT + 1)
-    run(2, QUERY_UNIT, QUERY_UNIT + 1, KEY_UNIT, VALUE_UNIT, UNITS)
+    run(4, 7, 2, 5, 8)
+    run(2, QUERY_UNIT, QUERY_UNIT + 1)
+    run(1, UNITS)
+    run(3, KEY_UNIT, VALUE_UNIT)
     run(4, OUT_UNIT, OUT_UNIT + 1)
-    run(3, QUERY_UNIT, QUERY_UNIT + 1, KEY_UNIT, VALUE_UNIT, UNITS)
-    run(4, QUERY_UNIT, QUERY_UNIT + 1, KEY_UNIT, VALUE_UNIT, UNITS)
+    run(2, UNITS)
+    run(3, QUERY_UNIT, QUERY_UNIT + 1, UNITS)
+    run(4, KEY_UNIT, VALUE_UNIT, QUERY_UNIT, QUERY_UNIT + 1, UNITS)
     run(5, *rest)
 
 
@@ -627,8 +706,8 @@
     wide = lambda *shape: pltpu.VMEM(shape, F32)
     sems = pltpu.SemaphoreType.DMA
     scratch = [
-        low(UNITS + 1, *BIG), low(6, *BIG), low(3, 512, 1024), low(1024, 128), wide(128, 1024), wide(128, 128), wide(128, 128),
-        low(128, 1024), low(1024, 128), low(128, 1024), low(128, 1024), low(8, 512, 128),
+        low(UNITS + 1, *BIG), low(6, *BIG), low(3, 512, 1024), low(128, 1024), wide(128, 1024), wide(512, 128), wide(512, 128),
+        low(4, 128, 1024), low(128, 1024), low(4, 512, 128),
         low(4, 128, 1024), low(4, 128, 1024), low(4, 128, 1024), low(4, 128, 128),
         low(1024, 512), low(1024, 512), wide(4, 128, 128), wide(512, 128), wide(512, 128),
         wide(4, 16, 128), wide(3, 16, 128), low(4, 128, 1024), low(3, 128, 1024),
@@ -642,7 +721,7 @@
         scratch += [low(count, 16, width), low(count, 16, width), low(count, 32, width), low(count, 32, width)]
         shared = count - EXPERT_UNITS if count == UNITS else 1
         scratch += [wide(shared, 32, width), wide(3, shared, 8, width)]
-    scratch += [sems((9, 3)), sems((9, 3)), sems((12, UNITS + 1)), sems((12, UNITS + 1)), sems((20,))]
+    scratch += [sems((48,)), sems((48,)), sems((12, UNITS + 1)), sems((12, UNITS + 1)), sems((20,))]
     shape = jax.ShapeDtypeStruct
     return pl.pallas_call(
         layer_kernel,
@@ -663,6 +742,40 @@
     )(*args)
 
 
+def place_kernel(
+    hidden_in, input_in, experts_in, shared_in, misc_in,
+    hidden_out, input_grad, attn_gain, query, key, value, out, ffn_gain, router, gate, up, down,
+):
+    hidden_out[...] = hidden_in[...]
+    input_grad[...] = input_in[...]
+    for kind, to in enumerate((gate, up, down)):
+        to[...] = experts_in[3 * kind : 3 * kind + 3]
+    key[...] = shared_in[KEY_UNIT - EXPERT_UNITS]
+    value[...] = shared_in[VALUE_UNIT - EXPERT_UNITS]
+    for part, lanes in ((0, slice(0, WIDE)), (1, slice(WIDE, 2 * WIDE))):
+        query[:, lanes] = shared_in[QUERY_UNIT - EXPERT_UNITS + part]
+        out[:, lanes] = shared_in[OUT_UNIT - EXPERT_UNITS + part]
+    router[...] = misc_in[:, 0:EXPERTS]
+    flipped = jnp.concatenate([misc_in[...], jnp.zeros((120, 128), F32)], axis=0).T
+    attn_gain[...] = flipped[EXPERTS : EXPERTS + 1, 0:8]
+    ffn_gain[...] = flipped[EXPERTS + 1 : EXPERTS + 2, 0:8]
+
+
+def place(*results):
+    vmem = pl.BlockSpec(memory_space=pltpu.VMEM)
+    shape = lambda *dims: jax.ShapeDtypeStruct(dims, F32)
+    return pl.pallas_call(
+        place_kernel,
+        out_shape=(
+            shape(128, 1024), shape(128, 1024), shape(1, 8), shape(8, 1024), shape(8, WIDE), shape(8, WIDE), shape(8, 1024),
+            shape(1, 8), shape(8, EXPERTS), shape(3, 32, WIDE), shape(3, 32, WIDE), shape(3, 32, WIDE),
+        ),
+        in_specs=[vmem] * 5,
+        out_specs=(vmem,) * 12,
+        name="place",
+    )(*results)
+
+
 def rope_tables(length):
     inverse = np.float32(10000.0) ** (-np.arange(32, dtype=np.float32) / np.float32(32))
     angles = np.arange(length, dtype=np.float32)[:, None] * inverse[None, :]
@@ -675,25 +788,15 @@
     w_gate, w_up, w_down, cotangent,
 ):
     cosine, sine = rope_tables(512)
-    hidden_out, input_grad, expert_done, shared, misc = layer(
-        tokens, routes[0], slot_order[0], prefix, attn_gain, ffn_gain, w_router[0],
+    results = layer(
+        tokens, routes[0].T, slot_order[0], prefix, attn_gain, ffn_gain, w_router[0].T,
         w_query.reshape(4, 4, 2, 32, 1024), w_key.reshape(BIG), w_value.reshape(BIG), w_out.reshape(4, 4, 2, 32, 1024),
         w_gate.reshape(3, *BIG), w_up.reshape(3, *BIG), w_down[0], cotangent, jnp.asarray(cosine), jnp.asarray(sine),
     )
-    at = lambda unit: unit - EXPERT_UNITS
+    hidden_out, input_grad, gain_attn, query, key, value, out, gain_ffn, router, gate, up, down = place(*results)
     return (
-        hidden_out,
-        input_grad,
-        misc[:, EXPERTS][None],
-        jnp.concatenate([shared[at(QUERY_UNIT)], shared[at(QUERY_UNIT + 1)]], axis=1)[None],
-        shared[at(KEY_UNIT)][None],
-        shared[at(VALUE_UNIT)][None],
-        jnp.concatenate([shared[at(OUT_UNIT)], shared[at(OUT_UNIT + 1)]], axis=1).T[None],
-        misc[:, EXPERTS + 1][None],
-        misc[:, :EXPERTS][None],
-        expert_done[0:3][None],
-        expert_done[3:6][None],
-        expert_done[6:9].transpose(0, 2, 1)[None],
+        hidden_out, input_grad, gain_attn, query[None], key[None], value[None], out.T[None], gain_ffn, router[None],
+        gate[None], up[None], down.transpose(0, 2, 1)[None],
     )
 
 

time: 155 us -> 125 us (0.81)
  Pallas kernels: 139 us -> 124 us
  local copies, waits for them, and re-layouts: 12.9 us -> 0 us
    pallas_call x1, Pallas kernels: 139 us -> 121 us  [layer(): pl.pallas_call(layer_kernel, out_shape=(shape((128, 1024), F32), shape((1...]
    unnamed x4 -> x0, local copies, waits for them, and re-layouts: 6.81 us -> none
    broadcast_in_dim x2 -> x0, local copies, waits for them, and re-layouts: 3.21 us -> none  [the longest x1 1.93 us: per_device(): expert_done[6:9].transpose(0, 2, 1)[None]]
    pallas_call x0 -> x1, Pallas kernels: none -> 2.65 us  [place(): pl.pallas_call(place_kernel, out_shape=(shape(128, 1024), shape(128, 1024...]
where the time goes in v1:
time: 125 us
  Pallas kernels  124 us (99%)
  between operations  1.33 us (1%)
    pallas_call x1, Pallas kernels, layer(): pl.pallas_call(layer_kernel, out_shape=(shape((128, 1024), F32), shape((1...  121 us
    pallas_call x1, Pallas kernels, place(): pl.pallas_call(place_kernel, out_shape=(shape(128, 1024), shape(128, 1024...  2.65 us

profile of v1, /device:TPU:0, one launch (start us, length us, event | category | flops | bytes accessed | tf_op | source)
XLA Modules:
  0.0 124.9 jit_solution(13559003036581678932)
XLA Ops:
  1.3 121.0 %layer.1 = (f32[128,1024]{1,0:T(8,128)}, f32[128,1024]{1,0:T(8,128)}, f32[9,32,512]{2,1,0:T(8,128)}, f32[6,8,512]{2,1,0:T(8,128)}, f32[8,128]{1,0:T(8,128)}) custom-call(bf16[128,1024]{1,0:T(8,128)(2,1)} %tokens.1, s32[8,128]{1,0:T(8,128)} %bitcast.34, s32[1,128]{1,0:T(1,128)} %bitcast.35, s32[1]{0:T(128)S(6)} %copy.29.prefix, f32[1,1024]{1,0:T(1,128)} %attn_gain.1, ...), custom_call_target="tpu_custom_call" | custom-call | tf_op jit(solution)/shard_map/layer/pallas_call | solution.py:726
  122.3 2.7 %place.1 = (f32[128,1024]{1,0:T(8,128)}, f32[128,1024]{1,0:T(8,128)}, f32[1,8]{1,0:T(1,128)}, f32[8,1024]{1,0:T(8,128)}, f32[8,512]{1,0:T(8,128)}, /*index=5*/f3...) custom-call(f32[128,1024]{1,0:T(8,128)} %get-tuple-element.29.hidden, ...), custom_call_target="tpu_custom_call" | custom-call | tf_op jit(solution)/shard_map/place/pallas_call | solution.py:767

commit v2 on v1

--- a/solution.py
+++ b/solution.py
@@ -14,10 +14,48 @@
 EXPERTS = 12
 OWN_EXPERTS = 3
 EXPERT_UNITS = 9
-UNITS = 15
-WIDE = 512
-KEY_UNIT, VALUE_UNIT, QUERY_UNIT, OUT_UNIT, SPARE = 9, 10, 11, 13, 15
+UNITS = 13
+WIDE, NARROW = 512, 384
+KEY_UNIT, VALUE_UNIT, OUT_UNIT = 9, 10, 11
+SLOTS = (0, 1, 2, 3, 4, 5, 6, 7, 8, 9, 10, 13, 14)
+PROBS, SLABS, SLOT_COUNT = 9, 11, 16
 BIG = (4, 4, 2, 32, WIDE)
+
+
+PLAN = (
+    (),
+    (),
+    (),
+    ((0, 0), (0, 3)),
+    ((0, 6),),
+    ((1, 0), (1, 3)),
+    (),
+    (),
+    ((1, 6), (0, 1)),
+    ((2, 3), (0, 4)),
+    ((0, 7), (2, 0)),
+    ((1, 1), (0, 2)),
+    (),
+    ((2, 6), (3, 3)),
+    ((0, 5), (0, 8)),
+    ((1, 4), (1, 7)),
+    ((3, 0), (1, 2)),
+    ((2, 1), (3, 6)),
+    ((4, 3), (0, 11)),
+    ((1, 5), (0, 12)),
+    ((1, 8), (2, 7)),
+    (),
+    (
+        (2, 4), (4, 0), (4, 6), (2, 2), (3, 1), (1, 11), (0, 9), (1, 12), (0, 10), (2, 5), (2, 8), (3, 7), (3, 4),
+        (4, 1), (0, 13), (3, 2), (2, 12), (2, 11),
+    ),
+    ((1, 10), (1, 9), (3, 5), (3, 8), (4, 7), (3, 11), (4, 4), (1, 13)),
+    ((2, 10), (4, 5), (4, 11), (4, 2), (3, 12), (2, 9), (4, 8)),
+    (
+        (6, 0), (2, 13), (5, 11), (3, 10), (3, 9), (4, 12), (3, 13), (4, 10), (4, 9), (6, 1), (4, 13), (5, 12),
+        (5, 10), (5, 9), (5, 13),
+    ),
+)
 
 
 def group_of(x_at, z_at, core):
@@ -87,12 +125,14 @@
 
 
 def layer_kernel(
-    tokens, routes, order, prefix, attn_gain, ffn_gain, w_router,
+    prefix, tokens_far, routes_far, order_far, attn_gain_far, ffn_gain_far, w_router_far,
     wq_far, wk_far, wv_far, wo_far, wg_far, wu_far, wd_far, cot_far, cos_far, sin_far,
-    hidden_out, input_grad, expert_out, shared_out, misc_out,
+    hidden_to, input_to, expert_to, query_to, key_to, value_to, out_to, misc_to,
+    hidden_out, input_grad, expert_out, query_out, key_out, value_out, out_out, misc_out,
+    tokens, routes, order, attn_gain, ffn_gain, w_router,
     grads, weights, wd, router, cot, cosine, sine,
     normed_all, joined, q_four, kv_all, x_all, g_all, code_all,
-    x_t, g_t, probs, gates, own_dots, dots_send, dots_in, row_send, row_in, mix_in, kvg_in,
+    x_t, g_t, probs, gates, own_dots, dots_send, dots_in, row_send, row_in, mix_in, q_low, q_all, grad_in,
     pair_in, lo_in, hi_in, minus_in, plus_in, lo_in_b, hi_in_b, minus_in_b, plus_in_b, last, last_in,
     misc, misc_pair, misc_lo, misc_hi, misc_minus, misc_plus, misc_lo_b, misc_hi_b, misc_minus_b, misc_plus_b,
     misc_last, misc_last_in,
@@ -103,7 +143,7 @@
     x_at, z_at, core = group // 8, (group // 2) % 4, group % 2
     spots = (x_at, z_at)
     own_rows = pl.ds(pl.multiple_of(y_at * 128, 128), 128)
-    middle, own_row, q_low, normed_t = hidden_out, input_grad, normed_all.at[y_at], g_t
+    middle, own_row, normed_t = hidden_out, input_grad, g_t
 
     def device(axis, offset):
         if axis == 0:
@@ -136,6 +176,12 @@
         for part in (0, 1):
             load((tag, at + part), src.at[:, :, :, :, half[part]], ref.at[to + part])
 
+    small = (
+        (tokens_far, tokens), (attn_gain_far, attn_gain), (routes_far, routes), (order_far, order),
+        (ffn_gain_far, ffn_gain), (w_router_far, w_router),
+    )
+    for at, (src, dst) in enumerate(small):
+        load(("small", at), src, dst)
     load_pair("fwd", 2, wq_far, grads, 2)
     load("cos", cos_far, cosine)
     load("sin", sin_far, sine)
@@ -145,7 +191,7 @@
         return ref[unit].reshape(1024, WIDE)
 
     def slab(index, rows=None):
-        unit, top = QUERY_UNIT + index // 2, (index % 2) * 2
+        unit, top = SLABS + index // 2, (index % 2) * 2
         if rows is None:
             return grads.at[unit, pl.ds(top, 2)]
         kind, at = rows
@@ -153,6 +199,8 @@
             return grads.at[unit, top + at]
         return grads.at[unit, top + at // 2, pl.ds((at % 2) * 2, 2)]
 
+    for at in (0, 1):
+        loads[("small", at)].wait()
     hidden = tokens[...].astype(F32)
     attn_r = lax.rsqrt(jnp.mean(hidden * hidden, axis=1, keepdims=True) + EPS)
     normed_all[y_at] = (hidden * attn_r * attn_gain[...]).astype(LOW)
@@ -204,19 +252,19 @@
             wait(self.second)
 
     class Scatter:
-        def __init__(self, block, land):
+        def __init__(self, spot, send, block, land):
             self.block, self.land = block, land
-            far = (y_at + 2) % 4
-            self.far = [y_copy(1, block(far, 0), land(0, 0)), y_copy(3, block(far, 1), land(0, 1))]
-            self.near = [y_copy(1, block(right, 1), land(1, 1)), y_copy(3, block(left, 0), land(2, 0))]
-            self.last = [y_copy(1, block(right, 0), land(1, 0)), y_copy(3, block(left, 1), land(2, 1))]
+            far, self.right, self.left = (spot + 2) % 4, (spot + 1) % 4, (spot + 3) % 4
+            self.far = [send(1, block(far, 0), land(0, 0)), send(3, block(far, 1), land(0, 1))]
+            self.near = [send(1, block(self.right, 1), land(1, 1)), send(3, block(self.left, 0), land(2, 0))]
+            self.last = [send(1, block(self.right, 0), land(1, 0)), send(3, block(self.left, 1), land(2, 1))]
 
         def start(self):
             start(self.far)
             start(self.near)
 
         def turn(self):
-            for part, to in ((0, right), (1, left)):
+            for part, to in ((0, self.right), (1, self.left)):
                 self.far[part].wait()
                 ref = self.block(to, part)
                 ref[...] = sum32(ref[...], self.land(0, part)[...])
@@ -234,7 +282,7 @@
     load("wu", wu_far, weights.at[pl.ds(3, 3)])
     load("wd", wd_far, wd)
 
-    for name in ("cos", "sin"):
+    for name in ("cos", "sin", ("small", 2), ("small", 3), ("small", 4), ("small", 5)):
         loads[name].wait()
     for part in (0, 1):
         loads[("fwd", 2 + part)].wait()
@@ -290,7 +338,7 @@
         return kv_all[:, :, lane_block(c + 4)].reshape(512, 128)
 
     def prob_ref(c):
-        return grads.at[KEY_UNIT + c // 2, pl.ds((c % 2) * 2, 2)]
+        return grads.at[PROBS + c // 2, pl.ds((c % 2) * 2, 2)]
 
     def attend(c):
         scores = jnp.where(visible(), dot_nt(key_block(c), q_four[c]) * 0.125, -1e30)
@@ -363,8 +411,144 @@
             slab(index)[:, :, :, :, lanes] = (outer * slope).astype(LOW).reshape(slab_shape)
 
     loop(2 * OWN_EXPERTS, expert_forward)
+    stand(x_all, x_t)
     g_share.finish()
-    loop(2 * OWN_EXPERTS, expert_back)
+    stand(g_all, g_t)
+    loop(2, expert_back)
+
+    class Wide:
+        src, pair, lo, hi, minus, plus = grads, pair_in, lo_in, hi_in, minus_in, plus_in
+        lo_b, hi_b, minus_b, plus_b = lo_in_b, hi_in_b, minus_in_b, plus_in_b
+
+    class Narrow:
+        src, pair, lo, hi, minus, plus = misc, misc_pair, misc_lo, misc_hi, misc_minus, misc_plus
+        lo_b, hi_b, minus_b, plus_b = misc_lo_b, misc_hi_b, misc_minus_b, misc_plus_b
+
+    class Unit:
+        def __init__(self, unit):
+            self.unit, self.axis, self.used = unit, unit % 2, 0
+            self.set, self.at = (Wide, unit) if unit < UNITS else (Narrow, 0)
+            s = self.set
+            ref = s.src.at[SLOTS[unit] if s is Wide else 0]
+            self.ref = ref
+            self.pair = self.remote(partner, ref.at[:, :, 1 - core], s.pair.at[self.at])
+
+            def block(index, part):
+                halves = pl.ds(2 * part, 2)
+                return ref.at[index, halves, core] if self.axis == 0 else ref.at[halves, index, core]
+
+            def land(at, part):
+                if at == 0:
+                    return (s.lo, s.hi)[part].at[self.at]
+                return (s.minus, s.plus)[at - 1].at[self.at, pl.ds(2 * part, 2)]
+
+            def cell(index, part=None):
+                place = ref.at[x_at, index, core] if self.axis == 0 else ref.at[index, z_at, core]
+                return place if part is None else place.at[pl.ds(16 * part, 16)]
+
+            def land_b(at, part):
+                if at == 0:
+                    return (s.lo_b, s.hi_b)[part].at[self.at]
+                return (s.minus_b, s.plus_b)[at - 1].at[self.at, pl.ds(16 * part, 16)]
+
+            axis = self.axis
+            self.ring = Scatter(spots[axis], lambda off, src, dst: self.remote(device(axis, off), src, dst), block, land)
+            self.ring_b = Scatter(spots[1 - axis], lambda off, src, dst: self.remote(device(1 - axis, off), src, dst), cell, land_b)
+            self.own = ref.at[spots[0], :, core] if axis == 0 else ref.at[:, spots[1], core]
+            self.own_b = cell(spots[1 - axis])
+            if unit >= EXPERT_UNITS:
+                src, dst, at = (last, last_in, unit - EXPERT_UNITS) if s is Wide else (misc_last, misc_last_in, 0)
+                self.last, self.last_in = src.at[at], [dst.at[off, at] for off in range(3)]
+                self.across = [
+                    self.remote(across(off), self.last.at[pl.ds((y_at + off) % 4 * 8, 8)], self.last_in[off - 1])
+                    for off in (1, 2, 3)
+                ]
+
+        def remote(self, to, src, dst):
+            self.used += 1
+            return pltpu.make_async_remote_copy(
+                src_ref=src, dst_ref=dst, send_sem=send_sem.at[self.unit, self.used - 1],
+                recv_sem=recv_sem.at[self.unit, self.used - 1], device_id=to, device_id_type=MESH,
+            )
+
+        def begin(self):
+            self.pair.start()
+
+        def after_pair(self):
+            s = self.set
+            self.pair.wait()
+            for slab_at in range(4):
+                ref = self.ref.at[slab_at, :, core]
+                ref[...] = sum32(ref[...], s.pair[self.at, slab_at])
+            self.ring.start()
+
+        def turn(self):
+            self.ring.turn()
+
+        def after_ring(self):
+            s = self.set
+            self.ring.finish()
+            total = self.own[...].astype(F32) + s.minus[self.at].astype(F32)
+            self.own[...] = (total + s.plus[self.at].astype(F32)).astype(LOW)
+            self.ring_b.start()
+
+        def turn_b(self):
+            self.ring_b.turn()
+
+        def after_ring_b(self):
+            s = self.set
+            self.ring_b.finish()
+            total = self.own_b[...].astype(F32) + s.minus_b[self.at].astype(F32)
+            total = total + s.plus_b[self.at].astype(F32)
+            if self.unit < EXPERT_UNITS:
+                expert_out[self.unit] = total
+            else:
+                self.last[...] = total
+                start(self.across)
+
+        def finish(self):
+            wait(self.across)
+            total = self.last[pl.ds(pl.multiple_of(y_at * 8, 8), 8), :]
+            if self.set is Narrow:
+                for off in range(4):
+                    rows = self.last_in[off - 1][:, 0:256] if off else total[:, 0:256]
+                    query_out[:, lane_block((y_at + 4 - off) % 4, 256)] = rows
+            for came in self.last_in:
+                total = total + came[...]
+            if self.unit == KEY_UNIT:
+                key_out[...] = total
+            elif self.unit == VALUE_UNIT:
+                value_out[...] = total
+            elif self.set is Wide:
+                out_out[:, half[self.unit - OUT_UNIT]] = total
+            else:
+                misc_out[...] = total[:, 256:]
+
+    extras = {}
+    stages = (Unit.after_pair, Unit.turn, Unit.after_ring, Unit.turn_b, Unit.after_ring_b, Unit.finish)
+    units = [Unit(unit) for unit in range(UNITS + 1)]
+
+    def run(point):
+        for stage, unit in PLAN[point]:
+            if stage < len(stages):
+                stages[stage](units[unit])
+            else:
+                extras[unit]()
+
+    def weight_grad(unit, left, right):
+        grads[SLOTS[unit]] = dot(left[...], right()).astype(LOW).reshape(BIG)
+        units[unit].begin()
+
+    def slab_value(index):
+        return lambda: slab(index)[...].reshape(512, WIDE)
+
+    def expert_units(j, point):
+        for at, (kind, turned_rows) in enumerate(((0, x_t), (3, x_t), (6, g_t))):
+            weight_grad(kind + j, turned_rows, slab_value(kind + j))
+            run(point + at)
+
+    expert_units(0, 0)
+    loop(2 * OWN_EXPERTS - 2, lambda step: expert_back(step + 2))
 
     dots_copies = [y_copy(off, dots_send.at[(y_at + off) % 4], dots_in.at[off - 1]) for off in (1, 3, 2)]
     for block in range(4):
@@ -387,172 +571,23 @@
     for off in (2, 1):
         row_send[across_block(off)] = rows[128 * (2 - off) : 128 * (3 - off)].astype(LOW)
     rows_back = Scatter(
-        lambda block, part: row_send.at[block, pl.ds(64 * part, 64)], lambda at, part: row_in.at[at, pl.ds(64 * part, 64)]
+        y_at, y_copy, lambda block, part: row_send.at[block, pl.ds(64 * part, 64)], lambda at, part: row_in.at[at, pl.ds(64 * part, 64)]
     )
     start(rows_back.far)
     rows_back.near[0].start()
+    run(3)
     rows = row_part(across_block(3), y_at)
     row_send[across_block(3)] = rows[0:128].astype(LOW)
     rows_back.near[1].start()
     own_row[...] = rows[128:256]
-    stand(x_all, x_t)
-    stand(g_all, g_t)
+    run(4)
     rows_back.turn()
     load_pair("bwd", 4, wo_far, weights, 3)
     load_pair("bwd", 2, wq_far, weights, 0)
     load_keys("bwd", weights, 2, 5)
 
-    class Wide:
-        src, pair, lo, hi, minus, plus = grads, pair_in, lo_in, hi_in, minus_in, plus_in
-        lo_b, hi_b, minus_b, plus_b = lo_in_b, hi_in_b, minus_in_b, plus_in_b
-
-    class Narrow:
-        src, pair, lo, hi, minus, plus = misc, misc_pair, misc_lo, misc_hi, misc_minus, misc_plus
-        lo_b, hi_b, minus_b, plus_b = misc_lo_b, misc_hi_b, misc_minus_b, misc_plus_b
-
-    def remote(unit, kind, src, dst, target):
-        return pltpu.make_async_remote_copy(
-            src_ref=src, dst_ref=dst, send_sem=send_sem.at[kind, unit], recv_sem=recv_sem.at[kind, unit],
-            device_id=target, device_id_type=MESH,
-        )
-
-    class Unit:
-        def __init__(self, unit):
-            self.unit = unit
-            self.set = Wide if unit < UNITS else Narrow
-            self.at = unit if unit < UNITS else 0
-            self.axis = unit % 2
-
-        def block(self, axis, index):
-            ref = self.set.src.at[self.at]
-            return ref.at[index, :, core] if axis == 0 else ref.at[:, index, core]
-
-        def cell(self, index):
-            ref = self.set.src.at[self.at]
-            return ref.at[x_at, index, core] if self.axis == 0 else ref.at[index, z_at, core]
-
-        def pair_copy(self):
-            s = self.set
-            return remote(self.unit, 0, s.src.at[self.at, :, :, 1 - core], s.pair.at[self.at], partner)
-
-        def far_copy(self, way):
-            s = self.set
-            src = self.block(self.axis, (spots[self.axis] + 2) % 4).at[pl.ds(2 * way, 2)]
-            dst = (s.lo, s.hi)[way].at[self.at]
-            return remote(self.unit, 1 + way, src, dst, device(self.axis, (1, 3)[way]))
-
-        def near_copy(self, way):
-            s = self.set
-            src = self.block(self.axis, (spots[self.axis] + (1, 3)[way]) % 4)
-            dst = (s.minus, s.plus)[way].at[self.at]
-            return remote(self.unit, 3 + way, src, dst, device(self.axis, (1, 3)[way]))
-
-        def far_copy_b(self, way):
-            s = self.set
-            src = self.cell((spots[1 - self.axis] + 2) % 4).at[pl.ds(16 * way, 16)]
-            dst = (s.lo_b, s.hi_b)[way].at[self.at]
-            return remote(self.unit, 5 + way, src, dst, device(1 - self.axis, (1, 3)[way]))
-
-        def near_copy_b(self, way):
-            s = self.set
-            src = self.cell((spots[1 - self.axis] + (1, 3)[way]) % 4)
-            dst = (s.minus_b, s.plus_b)[way].at[self.at]
-            return remote(self.unit, 7 + way, src, dst, device(1 - self.axis, (1, 3)[way]))
-
-        def across_copy(self, off):
-            to = (y_at + off) % 4
-            src, dst, at = (last, last_in, self.at - EXPERT_UNITS) if self.set is Wide else (misc_last, misc_last_in, 0)
-            return remote(self.unit, 8 + off, src.at[at, pl.ds(to * 8, 8)], dst.at[off - 1, at], across(off))
-
-        def begin(self):
-            self.pair_copy().start()
-
-        def after_pair(self):
-            s = self.set
-            self.pair_copy().wait()
-            for slab_at in range(4):
-                ref = s.src.at[self.at, slab_at, :, core]
-                ref[...] = sum32(ref[...], s.pair[self.at, slab_at])
-            self.far_copy(0).start()
-            self.far_copy(1).start()
-
-        def after_far(self):
-            s = self.set
-            for way in (0, 1):
-                self.far_copy(way).wait()
-                ref = self.block(self.axis, (spots[self.axis] + (1, 3)[way]) % 4).at[pl.ds(2 * way, 2)]
-                ref[...] = sum32(ref[...], (s.lo, s.hi)[way][self.at])
-                self.near_copy(way).start()
-
-        def after_near(self):
-            s = self.set
-            for way in (0, 1):
-                self.near_copy(way).wait()
-            ref = self.block(self.axis, spots[self.axis])
-            total = ref[...].astype(F32) + s.minus[self.at].astype(F32)
-            ref[...] = (total + s.plus[self.at].astype(F32)).astype(LOW)
-            for way in (0, 1):
-                self.far_copy_b(way).start()
-
-        def after_far_b(self):
-            s = self.set
-            for way in (0, 1):
-                self.far_copy_b(way).wait()
-                ref = self.cell((spots[1 - self.axis] + (1, 3)[way]) % 4).at[pl.ds(16 * way, 16)]
-                ref[...] = sum32(ref[...], (s.lo_b, s.hi_b)[way][self.at])
-                self.near_copy_b(way).start()
-
-        def after_near_b(self):
-            s = self.set
-            for way in (0, 1):
-                self.near_copy_b(way).wait()
-            total = self.cell(spots[1 - self.axis])[...].astype(F32) + s.minus_b[self.at].astype(F32)
-            total = total + s.plus_b[self.at].astype(F32)
-            if self.unit < EXPERT_UNITS:
-                expert_out[self.unit] = total
-                return
-            if self.set is Wide:
-                last[self.at - EXPERT_UNITS] = total
-            else:
-                misc_last[0] = total
-            for off in (1, 2, 3):
-                self.across_copy(off).start()
-
-        def finish(self):
-            for off in (1, 2, 3):
-                self.across_copy(off).wait()
-            src, dst, at = (last, last_in, self.at - EXPERT_UNITS) if self.set is Wide else (misc_last, misc_last_in, 0)
-            total = src[at, pl.ds(pl.multiple_of(y_at * 8, 8), 8), :]
-            for off in (1, 2, 3):
-                total = total + dst[off - 1, at]
-            if self.set is Wide:
-                shared_out[at] = total
-            else:
-                misc_out[...] = total
-
-    STAGES = ("after_pair", "after_far", "after_near", "after_far_b", "after_near_b", "finish")
-    units = [Unit(unit) for unit in range(UNITS + 1)]
-
-    def run(stage, *which):
-        for unit in which:
-            getattr(units[unit], STAGES[stage])()
-
-    def weight_grad(unit, left, right):
-        grads[unit] = dot(left[...], right()).astype(LOW).reshape(BIG)
-        units[unit].begin()
-
-    def slab_value(index):
-        return lambda: slab(index)[...].reshape(512, WIDE)
-
-    before_unit = None
-    for j in range(OWN_EXPERTS):
-        for kind, turned_rows in ((0, x_t), (3, x_t), (6, g_t)):
-            weight_grad(kind + j, turned_rows, slab_value(kind + j))
-            if before_unit is not None:
-                run(0, before_unit)
-            before_unit = kind + j
-    run(0, before_unit)
-    run(1, 0, 3, 6, 1)
+    expert_units(1, 5)
+    expert_units(2, 8)
 
     def mix_part(part):
         total = None
@@ -562,19 +597,19 @@
         x_all[pl.ds(part * 2, 2)] = total.astype(LOW).reshape(2, 128, 1024)
 
     loop(2, mix_part)
-    run(1, 4, 7)
+    run(11)
 
     def normed_stand(block):
         normed_t[:, lane_block(block)] = normed_all[block].T
 
     loop(4, normed_stand)
+    run(12)
 
     wait(dots_copies)
     rows_back.finish()
     mix_back = Scatter(
-        lambda block, part: x_all.at[block, pl.ds(64 * part, 64)], lambda at, part: mix_in.at[at, pl.ds(64 * part, 64)]
+        y_at, y_copy, lambda block, part: x_all.at[block, pl.ds(64 * part, 64)], lambda at, part: mix_in.at[at, pl.ds(64 * part, 64)]
     )
-    mix_back.start()
     taken = dots_send[y_at]
     moe_grad = own_row[...]
     for off in (1, 2, 3):
@@ -598,6 +633,7 @@
         loads[("bwd", 4 + part)].wait()
     head_grad = dot_nt(attn_grad[:, 0:WIDE], square(weights, 3)) + dot_nt(attn_grad[:, WIDE:], square(weights, 4))
     head_low = head_grad.astype(LOW).astype(F32)
+    run(13)
 
     def head_ref(c):
         return x_t.at[lane_block(c % 2, 512), lane_block(1 + c // 2)]
@@ -605,9 +641,11 @@
     for c in range(4):
         head_ref(c)[...] = four_heads(head_low[:, c * 256 : c * 256 + 128], head_low[:, c * 256 + 128 : c * 256 + 256])
     x_t[:, 0:128] = attn_grad.T
+    for part in (0, 1):
+        weight_grad(OUT_UNIT + part, x_t.at[:, pl.ds(0, 128)], lambda: joined[:, half[part]])
+    run(14)
 
     key_sums, value_sums = pair_in.at[0], pair_in.at[3]
-
     def attend_back(c):
         heads = head_ref(c)[...]
         low = prob_ref(c)[...].reshape(512, 512)
@@ -623,97 +661,104 @@
         q_low[:, lane_block(2 * c)] = turn(first, own_cosine, own_sine, -1.0).astype(LOW)
         q_low[:, lane_block(2 * c + 1)] = turn(second, own_cosine, own_sine, -1.0).astype(LOW)
 
-    loop(4, attend_back)
-    mix_back.turn()
-    kv_back = Scatter(lambda block, part: (key_sums, value_sums)[part].at[block], lambda at, part: kvg_in.at[at, part])
-    kv_back.start()
-
-    run(1, 2, 5, 8)
-    run(2, 0, 3, 6)
-    for part in (0, 1):
-        weight_grad(OUT_UNIT + part, x_t.at[:, pl.ds(0, 128)], lambda: joined[:, half[part]])
+    for c in range(4):
+        attend_back(c)
+        run(15 + c)
+    q_copies = [y_copy(off, q_low.at[:, lane_block(across_block(off), 256)], q_all.at[y_at]) for off in (1, 3, 2)]
+    start(q_copies)
+    q_all[y_at] = q_low[:, lane_block(y_at, 256)]
     weight_grad(KEY_UNIT, normed_t, lambda: key_sums[...].reshape(512, WIDE))
+    run(19)
     weight_grad(VALUE_UNIT, normed_t, lambda: value_sums[...].reshape(512, WIDE))
-    run(0, OUT_UNIT, OUT_UNIT + 1)
-    run(2, 1, 4)
-    for part in (0, 1):
-        weight_grad(QUERY_UNIT + part, normed_t.at[:, lane_block(y_at)], lambda: q_low[:, half[part]])
-    run(0, KEY_UNIT, VALUE_UNIT)
-    run(2, 7, 2, 5, 8)
-    run(1, OUT_UNIT, OUT_UNIT + 1)
-    run(0, QUERY_UNIT, QUERY_UNIT + 1)
+    run(20)
+
     for part in (0, 1, 2, 3):
         loads[("bwd", part)].wait()
-    normed_grad = dot_nt(q_low[:, 0:WIDE], square(weights, 0)) + dot_nt(q_low[:, WIDE:], square(weights, 1))
-    input_grad[...] = normed_grad
-    kv_back.turn()
-    mix_back.finish()
-    total = middle[...] + x_all[y_at].astype(F32)
-    for at in (1, 2):
-        total = total + mix_in[at].astype(F32)
-    hidden_out[...] = total
-    run(3, 0, 3, 6, 1, 4)
-    run(1, KEY_UNIT, VALUE_UNIT)
-    run(2, OUT_UNIT, OUT_UNIT + 1)
-    run(1, QUERY_UNIT, QUERY_UNIT + 1)
-    run(4, 0, 3, 6, 1, 4)
-
-    kv_back.finish()
-    key_back, value_back = key_sums[y_at].reshape(128, WIDE).astype(F32), value_sums[y_at].reshape(128, WIDE).astype(F32)
-    for at in (1, 2):
-        key_back = key_back + kvg_in[at, 0].reshape(128, WIDE).astype(F32)
-        value_back = value_back + kvg_in[at, 1].reshape(128, WIDE).astype(F32)
-    q_low[:, half[0]] = key_back.astype(LOW)
-    q_low[:, half[1]] = value_back.astype(LOW)
-    normed_grad = input_grad[...] + dot_nt(q_low[:, 0:WIDE], square(weights, 2))
-    normed_grad = normed_grad + dot_nt(q_low[:, WIDE:], square(weights, 5))
+    gain_rows = jnp.zeros((1, 1024), F32)
+    for part in (0, 1):
+        blocks = pl.ds(2 * part, 2)
+        rows = dot_nt(key_sums[blocks].reshape(256, WIDE), square(weights, 2))
+        rows = rows + dot_nt(value_sums[blocks].reshape(256, WIDE), square(weights, 5))
+        row_send[blocks] = rows.astype(LOW).reshape(2, 128, 1024)
+        scaled = rows * normed_all[blocks].reshape(256, 1024).astype(F32)
+        gain_rows = gain_rows + jnp.sum(scaled, axis=0, keepdims=True)
+    grad_back = Scatter(
+        y_at, y_copy, lambda block, part: row_send.at[block, pl.ds(64 * part, 64)], lambda at, part: grad_in.at[at, pl.ds(64 * part, 64)]
+    )
+    grad_back.start()
+    rows = dot_nt(q_low[:, 0:WIDE], square(weights, 0)) + dot_nt(q_low[:, WIDE:], square(weights, 1))
+    input_grad[...] = rows
+    gain_rows = gain_rows + jnp.sum(rows * normed_all[y_at].astype(F32), axis=0, keepdims=True)
+    wide_lane = lanes_of((1024, 128))
+    gains = jnp.where(
+        wide_lane == EXPERTS,
+        jnp.broadcast_to(gain_rows / attn_gain[...], (128, 1024)).T,
+        jnp.broadcast_to(ffn_gain_grad, (128, 1024)).T,
+    )
+    gains = jnp.where(wide_lane < EXPERTS, router_grad, gains).astype(LOW)
+    misc[0, :, :, :, :, 256:] = gains.reshape(4, 4, 2, 32, 128)
+    run(21)
+    wait(q_copies)
+    misc[0, :, :, :, :, 0:256] = dot(normed_t[...], q_all[...].reshape(512, 256)).astype(LOW).reshape(4, 4, 2, 32, 256)
+    units[UNITS].begin()
+    run(22)
+    grad_back.turn()
+    mix_back.start()
+    run(23)
+
+    grad_back.finish()
+    normed_grad = input_grad[...] + row_send[y_at].astype(F32) + grad_in[1].astype(F32) + grad_in[2].astype(F32)
     hidden = tokens[...].astype(F32)
     attn_r = lax.rsqrt(jnp.mean(hidden * hidden, axis=1, keepdims=True) + EPS)
     scaled = normed_grad * attn_gain[...]
-    attn_gain_grad = jnp.sum(normed_grad * hidden * attn_r, axis=0, keepdims=True)
     shrink = attn_r * attn_r * attn_r * jnp.mean(scaled * hidden, axis=1, keepdims=True)
     input_grad[...] = cot[...] + attn_r * scaled - hidden * shrink
-    wide_lane = lanes_of((1024, 128))
-    gains = jnp.where(
-        wide_lane == EXPERTS,
-        jnp.broadcast_to(attn_gain_grad, (128, 1024)).T,
-        jnp.broadcast_to(ffn_gain_grad, (128, 1024)).T,
-    )
-    misc[0] = jnp.where(wide_lane < EXPERTS, router_grad, gains).astype(LOW).reshape(4, 4, 2, 32, 128)
-    units[UNITS].begin()
-
-    rest = (OUT_UNIT, OUT_UNIT + 1, QUERY_UNIT, QUERY_UNIT + 1, KEY_UNIT, VALUE_UNIT, UNITS)
-    run(3, 7, 2, 5, 8)
-    run(2, KEY_UNIT, VALUE_UNIT)
-    run(0, UNITS)
-    run(3, OUT_UNIT, OUT_UNIT + 1)
-    run(4, 7, 2, 5, 8)
-    run(2, QUERY_UNIT, QUERY_UNIT + 1)
-    run(1, UNITS)
-    run(3, KEY_UNIT, VALUE_UNIT)
-    run(4, OUT_UNIT, OUT_UNIT + 1)
-    run(2, UNITS)
-    run(3, QUERY_UNIT, QUERY_UNIT + 1, UNITS)
-    run(4, KEY_UNIT, VALUE_UNIT, QUERY_UNIT, QUERY_UNIT + 1, UNITS)
-    run(5, *rest)
+    results = {}
+
+    def result(src, dst):
+        copy = pltpu.make_async_copy(src, dst, local_sem.at[len(loads) + len(results)])
+        results[len(results)] = copy
+        copy.start()
+
+    result(input_grad, input_to)
+
+    def finish_mix():
+        mix_back.finish()
+        total = middle[...] + x_all[y_at].astype(F32)
+        for at in (1, 2):
+            total = total + mix_in[at].astype(F32)
+        hidden_out[...] = total
+        result(hidden_out, hidden_to)
+
+    extras[0] = mix_back.turn
+    extras[1] = finish_mix
+    run(24)
+    result(expert_out, expert_to)
+    run(25)
+    for src, dst in ((query_out, query_to), (key_out, key_to), (value_out, value_to), (out_out, out_to), (misc_out, misc_to)):
+        result(src, dst)
+    wait(results.values())
 
 
 def layer(*args):
-    vmem = pl.BlockSpec(memory_space=pltpu.VMEM)
     smem = pl.BlockSpec(memory_space=pltpu.SMEM)
     far = pl.BlockSpec(memory_space=pl.ANY)
     low = lambda *shape: pltpu.VMEM(shape, LOW)
     wide = lambda *shape: pltpu.VMEM(shape, F32)
     sems = pltpu.SemaphoreType.DMA
     scratch = [
-        low(UNITS + 1, *BIG), low(6, *BIG), low(3, 512, 1024), low(128, 1024), wide(128, 1024), wide(512, 128), wide(512, 128),
+        wide(128, 1024), wide(128, 1024), wide(EXPERT_UNITS, 32, WIDE),
+        wide(8, 1024), wide(8, WIDE), wide(8, WIDE), wide(8, 1024), wide(8, 128),
+        low(128, 1024), pltpu.VMEM((8, 128), jnp.int32), pltpu.VMEM((1, 128), jnp.int32),
+        wide(1, 1024), wide(1, 1024), low(EXPERTS, 1024),
+        low(SLOT_COUNT, *BIG), low(6, *BIG), low(3, 512, 1024), low(128, 1024), wide(128, 1024), wide(512, 128), wide(512, 128),
         low(4, 128, 1024), low(128, 1024), low(4, 512, 128),
         low(4, 128, 1024), low(4, 128, 1024), low(4, 128, 1024), low(4, 128, 128),
         low(1024, 512), low(1024, 512), wide(4, 128, 128), wide(512, 128), wide(512, 128),
-        wide(4, 16, 128), wide(3, 16, 128), low(4, 128, 1024), low(3, 128, 1024),
-        low(3, 128, 1024), low(3, 2, 4, 32, WIDE),
+        wide(4, 16, 128), wide(3, 16, 128), low(4, 128, 1024), low(3, 128, 1024), low(3, 128, 1024),
+        low(128, 1024), low(4, 128, 256), low(3, 128, 1024),
     ]
-    for count, width in ((UNITS, WIDE), (1, 128)):
+    for count, width in ((UNITS, WIDE), (1, NARROW)):
         if count == 1:
             scratch += [low(1, 4, 4, 2, 32, width)]
         scratch += [low(count, 4, 4, 32, width), low(count, 2, 32, width), low(count, 2, 32, width)]
@@ -721,7 +766,7 @@
         scratch += [low(count, 16, width), low(count, 16, width), low(count, 32, width), low(count, 32, width)]
         shared = count - EXPERT_UNITS if count == UNITS else 1
         scratch += [wide(shared, 32, width), wide(3, shared, 8, width)]
-    scratch += [sems((48,)), sems((48,)), sems((12, UNITS + 1)), sems((12, UNITS + 1)), sems((20,))]
+    scratch += [sems((48,)), sems((48,)), sems((UNITS + 1, 16)), sems((UNITS + 1, 16)), sems((32,))]
     shape = jax.ShapeDtypeStruct
     return pl.pallas_call(
         layer_kernel,
@@ -729,11 +774,14 @@
             shape((128, 1024), F32),
             shape((128, 1024), F32),
             shape((EXPERT_UNITS, 32, WIDE), F32),
-            shape((UNITS - EXPERT_UNITS, 8, WIDE), F32),
+            shape((8, 1024), F32),
+            shape((8, WIDE), F32),
+            shape((8, WIDE), F32),
+            shape((8, 1024), F32),
             shape((8, 128), F32),
         ),
-        in_specs=[vmem, vmem, vmem, smem, vmem, vmem, vmem] + [far] * 10,
-        out_specs=(vmem,) * 5,
+        in_specs=[smem] + [far] * 16,
+        out_specs=(far,) * 8,
         scratch_shapes=scratch,
         compiler_params=pltpu.CompilerParams(
             collective_id=0, has_side_effects=True, vmem_limit_bytes=60 * 2**20
@@ -743,18 +791,15 @@
 
 
 def place_kernel(
-    hidden_in, input_in, experts_in, shared_in, misc_in,
+    hidden_in, input_in, experts_in, query_in, key_in, value_in, out_in, misc_in,
     hidden_out, input_grad, attn_gain, query, key, value, out, ffn_gain, router, gate, up, down,
 ):
     hidden_out[...] = hidden_in[...]
     input_grad[...] = input_in[...]
     for kind, to in enumerate((gate, up, down)):
         to[...] = experts_in[3 * kind : 3 * kind + 3]
-    key[...] = shared_in[KEY_UNIT - EXPERT_UNITS]
-    value[...] = shared_in[VALUE_UNIT - EXPERT_UNITS]
-    for part, lanes in ((0, slice(0, WIDE)), (1, slice(WIDE, 2 * WIDE))):
-        query[:, lanes] = shared_in[QUERY_UNIT - EXPERT_UNITS + part]
-        out[:, lanes] = shared_in[OUT_UNIT - EXPERT_UNITS + part]
+    for src, to in ((query_in, query), (key_in, key), (value_in, value), (out_in, out)):
+        to[...] = src[...]
     router[...] = misc_in[:, 0:EXPERTS]
     flipped = jnp.concatenate([misc_in[...], jnp.zeros((120, 128), F32)], axis=0).T
     attn_gain[...] = flipped[EXPERTS : EXPERTS + 1, 0:8]
@@ -770,7 +815,7 @@
             shape(128, 1024), shape(128, 1024), shape(1, 8), shape(8, 1024), shape(8, WIDE), shape(8, WIDE), shape(8, 1024),
             shape(1, 8), shape(8, EXPERTS), shape(3, 32, WIDE), shape(3, 32, WIDE), shape(3, 32, WIDE),
         ),
-        in_specs=[vmem] * 5,
+        in_specs=[vmem] * 8,
         out_specs=(vmem,) * 12,
         name="place",
     )(*results)
@@ -789,7 +834,7 @@
 ):
     cosine, sine = rope_tables(512)
     results = layer(
-        tokens, routes[0].T, slot_order[0], prefix, attn_gain, ffn_gain, w_router[0].T,
+        prefix, tokens, routes[0].T, slot_order[0], attn_gain, ffn_gain, w_router[0].T,
         w_query.reshape(4, 4, 2, 32, 1024), w_key.reshape(BIG), w_value.reshape(BIG), w_out.reshape(4, 4, 2, 32, 1024),
         w_gate.reshape(3, *BIG), w_up.reshape(3, *BIG), w_down[0], cotangent, jnp.asarray(cosine), jnp.asarray(sine),
     )

time: 125 us -> 115 us (0.920)
  Pallas kernels: 124 us -> 113 us
    pallas_call x1, Pallas kernels: 121 us -> 110 us  [layer(): pl.pallas_call(layer_kernel, out_shape=(shape((128, 1024), F32), shape((1...]
where the time goes in v2:
time: 115 us
  Pallas kernels  113 us (98%)
  between operations  1.36 us (1%)
    pallas_call x1, Pallas kernels, layer(): pl.pallas_call(layer_kernel, out_shape=(shape((128, 1024), F32), shape((1...  110 us
    pallas_call x1, Pallas kernels, place(): pl.pallas_call(place_kernel, out_shape=(shape(128, 1024), shape(128, 1024...  2.68 us

profile of v2, /device:TPU:0, one launch (start us, length us, event | category | flops | bytes accessed | tf_op | source)
XLA Modules:
  0.0 114.5 jit_solution(12054254616815463176)
XLA Ops:
  1.3 110.5 %layer.1 = (f32[128,1024]{1,0:T(8,128)}, f32[128,1024]{1,0:T(8,128)}, f32[9,32,512]{2,1,0:T(8,128)}, f32[8,1024]{1,0:T(8,128)}, f32[8,512]{1,0:T(8,128)}, /*inde...) custom-call(s32[1]{0:T(128)S(6)} %copy.29.prefix, bf16[128,1024]{1,0:T(8,128)(2,1)} %tokens_far.1, ...), custom_call_target="tpu_custom_call" | custom-call | tf_op jit(solution)/shard_map/layer/pallas_call | solution.py:771
  111.8 2.7 %place.1 = (f32[128,1024]{1,0:T(8,128)}, f32[128,1024]{1,0:T(8,128)}, f32[1,8]{1,0:T(1,128)}, f32[8,1024]{1,0:T(8,128)}, f32[8,512]{1,0:T(8,128)}, /*index=5*/f3...) custom-call(f32[128,1024]{1,0:T(8,128)} %get-tuple-element.32.hidden, ...), custom_call_target="tpu_custom_call" | custom-call | tf_op jit(solution)/shard_map/place/pallas_call | solution.py:812

commit v3 on v2

--- a/solution.py
+++ b/solution.py
@@ -16,7 +16,7 @@
 EXPERT_UNITS = 9
 UNITS = 13
 WIDE, NARROW = 512, 384
-KEY_UNIT, VALUE_UNIT, OUT_UNIT = 9, 10, 11
+KV_UNIT, OUT_UNIT = 9, 11
 SLOTS = (0, 1, 2, 3, 4, 5, 6, 7, 8, 9, 10, 13, 14)
 PROBS, SLABS, SLOT_COUNT = 9, 11, 16
 BIG = (4, 4, 2, 32, WIDE)
@@ -26,35 +26,36 @@
     (),
     (),
     (),
-    ((0, 0), (0, 3)),
-    ((0, 6),),
-    ((1, 0), (1, 3)),
-    (),
-    (),
-    ((1, 6), (0, 1)),
-    ((2, 3), (0, 4)),
-    ((0, 7), (2, 0)),
-    ((1, 1), (0, 2)),
-    (),
-    ((2, 6), (3, 3)),
-    ((0, 5), (0, 8)),
+    ((0, 0),),
+    ((0, 3), (0, 6)),
+    (),
+    (),
+    ((1, 0),),
+    (),
+    (),
+    (),
+    ((1, 3), (0, 1)),
+    ((1, 6), (0, 4), (0, 7), (2, 0), (0, 2), (0, 5)),
+    ((2, 3), (0, 8)),
+    ((2, 6), (1, 1)),
     ((1, 4), (1, 7)),
-    ((3, 0), (1, 2)),
-    ((2, 1), (3, 6)),
-    ((4, 3), (0, 11)),
-    ((1, 5), (0, 12)),
-    ((1, 8), (2, 7)),
-    (),
+    ((1, 2),),
+    ((5, 0),),
+    ((0, 11), (5, 3)),
+    (),
+    ((0, 12), (1, 5), (1, 8)),
+    ((2, 1), (2, 4)),
     (
-        (2, 4), (4, 0), (4, 6), (2, 2), (3, 1), (1, 11), (0, 9), (1, 12), (0, 10), (2, 5), (2, 8), (3, 7), (3, 4),
-        (4, 1), (0, 13), (3, 2), (2, 12), (2, 11),
+        (0, 10), (1, 11), (1, 12), (2, 7), (2, 2), (0, 13), (1, 9), (3, 0), (3, 3), (2, 5), (2, 8), (1, 10),
+        (5, 1), (5, 4), (3, 6),
     ),
-    ((1, 10), (1, 9), (3, 5), (3, 8), (4, 7), (3, 11), (4, 4), (1, 13)),
-    ((2, 10), (4, 5), (4, 11), (4, 2), (3, 12), (2, 9), (4, 8)),
-    (
-        (6, 0), (2, 13), (5, 11), (3, 10), (3, 9), (4, 12), (3, 13), (4, 10), (4, 9), (6, 1), (4, 13), (5, 12),
-        (5, 10), (5, 9), (5, 13),
-    ),
+    ((2, 12), (2, 11), (1, 13), (5, 7), (5, 2), (2, 10), (5, 5), (2, 9), (3, 1)),
+    ((3, 11), (5, 8), (3, 12), (2, 13), (3, 9), (3, 10), (3, 7), (3, 4), (3, 13), (3, 5), (3, 2), (3, 8)),
+    ((6, 1), (4, 11), (4, 12), (4, 9), (4, 10), (4, 13)),
+    (),
+    (),
+    ((6, 0), (5, 6)),
+    ((0, 9),),
 )
 
 
@@ -74,8 +75,8 @@
     return lax.dot_general(first, second, (((0,), (0,)), ((), ())), preferred_element_type=F32)
 
 
-def sum32(first, second):
-    return (first.astype(F32) + second.astype(F32)).astype(LOW)
+def add(first, second):
+    return first + second
 
 
 def lanes_of(shape):
@@ -131,10 +132,10 @@
     hidden_out, input_grad, expert_out, query_out, key_out, value_out, out_out, misc_out,
     tokens, routes, order, attn_gain, ffn_gain, w_router,
     grads, weights, wd, router, cot, cosine, sine,
-    normed_all, joined, q_four, kv_all, x_all, g_all, code_all,
+    normed_all, joined, q_four, kv_all, x_all, g_all, code_all, codes,
     x_t, g_t, probs, gates, own_dots, dots_send, dots_in, row_send, row_in, mix_in, q_low, q_all, grad_in,
-    pair_in, lo_in, hi_in, minus_in, plus_in, lo_in_b, hi_in_b, minus_in_b, plus_in_b, last, last_in,
-    misc, misc_pair, misc_lo, misc_hi, misc_minus, misc_plus, misc_lo_b, misc_hi_b, misc_minus_b, misc_plus_b,
+    pair_in, lo_in, hi_in, minus_in, plus_in, cells_in, last, last_in,
+    misc, misc_pair, misc_lo, misc_hi, misc_minus, misc_plus, misc_cells,
     misc_last, misc_last_in,
     y_send, y_recv, send_sem, recv_sem, local_sem,
 ):
@@ -204,6 +205,18 @@
     hidden = tokens[...].astype(F32)
     attn_r = lax.rsqrt(jnp.mean(hidden * hidden, axis=1, keepdims=True) + EPS)
     normed_all[y_at] = (hidden * attn_r * attn_gain[...]).astype(LOW)
+    for at in (2, 3):
+        loads[("small", at)].wait()
+    expert_at = lax.broadcasted_iota(jnp.int32, (128, 128), 0)
+    member = jnp.zeros((128, 128), F32)
+    for pick in range(routes.shape[0]):
+        member = member + jnp.where(routes[pick : pick + 1, :] == expert_at, 1.0, 0.0)
+    member = member.T
+    ranks = jnp.broadcast_to(order[...].astype(F32), (128, 128))
+    earlier = jnp.where(ranks < ranks.T, 1.0, 0.0).astype(LOW)
+    before = dot(earlier, member.astype(LOW))
+    code = jnp.where((member > 0.5) & (before < CAP - 0.5), 2.0, member)
+    code_all[y_at] = code.T[0:16].astype(LOW)
     pl.semaphore_wait(barrier, len(peers))
 
     y_used = []
@@ -244,9 +257,11 @@
                 came.wait_recv()
                 on.start()
 
-        def finish(self):
+        def near(self):
             for copy in self.first[2:]:
                 copy.wait_recv()
+
+        def finish(self):
             for copy in self.first:
                 copy.wait_send()
             wait(self.second)
@@ -267,7 +282,7 @@
             for part, to in ((0, self.right), (1, self.left)):
                 self.far[part].wait()
                 ref = self.block(to, part)
-                ref[...] = sum32(ref[...], self.land(0, part)[...])
+                ref[...] = add(ref[...], self.land(0, part)[...])
                 self.last[part].start()
 
         def finish(self):
@@ -276,13 +291,15 @@
 
     normed_share = Gather(normed_all)
     normed_share.start()
+    code_share = [y_copy(off, code_all.at[y_at], code_all.at[y_at]) for off in (1, 3, 2)]
+    start(code_share)
     load_pair("fwd", 4, wo_far, grads, 4)
     load("cot", cot_far, cot)
     load("wg", wg_far, weights.at[pl.ds(0, 3)])
     load("wu", wu_far, weights.at[pl.ds(3, 3)])
     load("wd", wd_far, wd)
 
-    for name in ("cos", "sin", ("small", 2), ("small", 3), ("small", 4), ("small", 5)):
+    for name in ("cos", "sin", ("small", 4), ("small", 5)):
         loads[name].wait()
     for part in (0, 1):
         loads[("fwd", 2 + part)].wait()
@@ -293,15 +310,6 @@
                 turned[:, c * 256 : c * 256 + 128], turned[:, c * 256 + 128 : c * 256 + 256]
             )
 
-    expert_at = lax.broadcasted_iota(jnp.int32, (128, 128), 0)
-    member = jnp.zeros((128, 128), F32)
-    for pick in range(routes.shape[0]):
-        member = member + jnp.where(routes[pick : pick + 1, :] == expert_at, 1.0, 0.0)
-    member = member.T
-    ranks = jnp.broadcast_to(order[...].astype(F32), (128, 128))
-    earlier = jnp.where(ranks < ranks.T, 1.0, 0.0).astype(LOW)
-    before = dot(earlier, member.astype(LOW))
-    code_all[y_at] = jnp.where((member > 0.5) & (before < CAP - 0.5), 2.0, member).astype(LOW)
     loads["cot"].wait()
     g_all[y_at] = cot[...].astype(LOW)
     router[...] = jnp.zeros_like(router)
@@ -309,6 +317,9 @@
     for part in (0, 1):
         loads[("fwd", part)].wait()
     normed_share.forward()
+    g_share = Gather(g_all)
+    g_share.start()
+    normed_share.near()
     normed_share.finish()
 
     def keys_values(part):
@@ -320,10 +331,6 @@
         kv_all[:, :, lane_block(2 + part, 256)] = values.astype(LOW).reshape(4, 128, 256)
 
     loop(2, keys_values)
-    g_share = Gather(g_all)
-    g_share.start()
-    code_share = [y_copy(off, code_all.at[y_at], code_all.at[y_at]) for off in (1, 3, 2)]
-    start(code_share)
 
     def visible():
         shape = (512, 512)
@@ -360,6 +367,9 @@
     x_share.start()
 
     wait(code_share)
+    for block in range(4):
+        short = code_all[block].astype(F32)
+        codes[block] = jnp.concatenate([short, jnp.zeros((112, 128), F32)], axis=0).T
 
     def stand(ref, out):
         def body(block):
@@ -368,36 +378,52 @@
         loop(4, body)
 
     x_share.forward()
-    x_share.finish()
     g_share.forward()
-
-    code = code_all[...].reshape(512, 128).astype(F32)
-    in_use = code > 0.5
-    logits = jnp.where(in_use, dot_nt(x_all[...].reshape(512, 1024), router[...]), -1e30)
-    raised = jnp.where(in_use, jnp.exp(logits - jnp.max(logits, axis=1, keepdims=True)), 0.0)
-    soft = raised / jnp.sum(raised, axis=1, keepdims=True)
-    probs[...] = soft.reshape(4, 128, 128)
-    gates[...] = jnp.where(code > 1.5, soft, 0.0)
-    own_dots[...] = jnp.zeros_like(own_dots)
     for name in ("wg", "wu", "wd"):
         loads[name].wait()
     slab_shape = (2, 4, 2, 32, 256)
 
-    def gate_of(j):
-        here = lanes_of((512, 128)) == y_at * OWN_EXPERTS + j
-        return here, jnp.sum(jnp.where(here, gates[...], 0.0), axis=1, keepdims=True)
-
-    def expert_forward(step):
-        j, lanes = step // 2, lane_block(step % 2, 256)
-        inputs = x_all[...].reshape(512, 1024)
-        gate_lin = dot(inputs, weights[j, :, :, :, :, lanes].reshape(1024, 256))
-        up_lin = dot(inputs, weights[3 + j, :, :, :, :, lanes].reshape(1024, 256))
-        sig = 1.0 / (1.0 + jnp.exp(-gate_lin))
-        silu = gate_lin * sig
-        act = (silu * up_lin).astype(LOW).astype(F32) * gate_of(j)[1]
-        slab(6 + j)[:, :, :, :, lanes] = act.astype(LOW).reshape(slab_shape)
-        slab(j)[:, :, :, :, lanes] = (up_lin * sig * (1.0 + gate_lin * (1.0 - sig))).astype(LOW).reshape(slab_shape)
-        slab(3 + j)[:, :, :, :, lanes] = silu.astype(LOW).reshape(slab_shape)
+    def gate_of(j, rows=pl.ds(0, 512), count=512):
+        here = lanes_of((count, 128)) == y_at * OWN_EXPERTS + j
+        return here, jnp.sum(jnp.where(here, gates[rows, :], 0.0), axis=1, keepdims=True)
+
+    def expert_forward(blocks):
+        def rows_of(ref):
+            return jnp.concatenate([ref[block] for block in blocks], axis=0)
+
+        code = rows_of(codes)
+        in_use = code > 0.5
+        logits = jnp.where(in_use, dot_nt(rows_of(x_all), router[...]), -1e30)
+        raised = jnp.where(in_use, jnp.exp(logits - jnp.max(logits, axis=1, keepdims=True)), 0.0)
+        soft = raised / jnp.sum(raised, axis=1, keepdims=True)
+        kept = jnp.where(code > 1.5, soft, 0.0)
+        for at, block in enumerate(blocks):
+            probs[block] = soft[128 * at : 128 * at + 128]
+            gates[lane_block(block), :] = kept[128 * at : 128 * at + 128]
+
+        def body(step):
+            j, lanes = step // 2, lane_block(step % 2, 256)
+            inputs = rows_of(x_all)
+            gate_lin = dot(inputs, weights[j, :, :, :, :, lanes].reshape(1024, 256))
+            up_lin = dot(inputs, weights[3 + j, :, :, :, :, lanes].reshape(1024, 256))
+            sig = 1.0 / (1.0 + jnp.exp(-gate_lin))
+            silu = gate_lin * sig
+            gate = jnp.concatenate([gate_of(j, lane_block(block), 128)[1] for block in blocks], axis=0)
+            act = (silu * up_lin).astype(LOW).astype(F32) * gate
+            slope = up_lin * sig * (1.0 + gate_lin * (1.0 - sig))
+            for index, value in ((6 + j, act), (j, slope), (3 + j, silu)):
+                value = value.astype(LOW)
+                for at, block in enumerate(blocks):
+                    piece = value[128 * at : 128 * at + 128].reshape(2, 2, 32, 256)
+                    slab(index, (128, block))[:, :, :, lanes] = piece
+
+        loop(2 * OWN_EXPERTS, body)
+
+    own_dots[...] = jnp.zeros_like(own_dots)
+    x_share.near()
+    expert_forward((y_at, left, right))
+    x_share.finish()
+    expert_forward(((y_at + 2) % 4,))
 
     def expert_back(step):
         j, lanes = step // 2, lane_block(step % 2, 256)
@@ -410,19 +436,19 @@
             slope = slab(index)[:, :, :, :, lanes].reshape(512, 256).astype(F32)
             slab(index)[:, :, :, :, lanes] = (outer * slope).astype(LOW).reshape(slab_shape)
 
-    loop(2 * OWN_EXPERTS, expert_forward)
     stand(x_all, x_t)
+    g_share.near()
     g_share.finish()
     stand(g_all, g_t)
     loop(2, expert_back)
 
     class Wide:
         src, pair, lo, hi, minus, plus = grads, pair_in, lo_in, hi_in, minus_in, plus_in
-        lo_b, hi_b, minus_b, plus_b = lo_in_b, hi_in_b, minus_in_b, plus_in_b
+        cells = cells_in
 
     class Narrow:
         src, pair, lo, hi, minus, plus = misc, misc_pair, misc_lo, misc_hi, misc_minus, misc_plus
-        lo_b, hi_b, minus_b, plus_b = misc_lo_b, misc_hi_b, misc_minus_b, misc_plus_b
+        cells = misc_cells
 
     class Unit:
         def __init__(self, unit):
@@ -442,20 +468,26 @@
                     return (s.lo, s.hi)[part].at[self.at]
                 return (s.minus, s.plus)[at - 1].at[self.at, pl.ds(2 * part, 2)]
 
-            def cell(index, part=None):
-                place = ref.at[x_at, index, core] if self.axis == 0 else ref.at[index, z_at, core]
-                return place if part is None else place.at[pl.ds(16 * part, 16)]
-
-            def land_b(at, part):
-                if at == 0:
-                    return (s.lo_b, s.hi_b)[part].at[self.at]
-                return (s.minus_b, s.plus_b)[at - 1].at[self.at, pl.ds(16 * part, 16)]
+            def cell(index):
+                return ref.at[x_at, index, core] if self.axis == 0 else ref.at[index, z_at, core]
 
             axis = self.axis
             self.ring = Scatter(spots[axis], lambda off, src, dst: self.remote(device(axis, off), src, dst), block, land)
-            self.ring_b = Scatter(spots[1 - axis], lambda off, src, dst: self.remote(device(1 - axis, off), src, dst), cell, land_b)
+            spot = spots[1 - axis]
+            self.cell, self.cells_in = cell(spot), [s.cells.at[off, self.at] for off in range(3)]
+            self.direct = unit >= EXPERT_UNITS
+            if self.direct:
+                self.cells = [
+                    self.remote(device(1 - axis, off), cell((spot + off) % 4), self.cells_in[off - 1]) for off in (1, 3, 2)
+                ]
+            else:
+                self.ring_b = Scatter(
+                    spot,
+                    lambda off, src, dst: self.remote(device(1 - axis, off), src, dst),
+                    lambda index, part: cell(index).at[pl.ds(16 * part, 16)],
+                    lambda at, part: self.cells_in[at].at[pl.ds(16 * part, 16)],
+                )
             self.own = ref.at[spots[0], :, core] if axis == 0 else ref.at[:, spots[1], core]
-            self.own_b = cell(spots[1 - axis])
             if unit >= EXPERT_UNITS:
                 src, dst, at = (last, last_in, unit - EXPERT_UNITS) if s is Wide else (misc_last, misc_last_in, 0)
                 self.last, self.last_in = src.at[at], [dst.at[off, at] for off in range(3)]
@@ -479,7 +511,7 @@
             self.pair.wait()
             for slab_at in range(4):
                 ref = self.ref.at[slab_at, :, core]
-                ref[...] = sum32(ref[...], s.pair[self.at, slab_at])
+                ref[...] = add(ref[...], s.pair[self.at, slab_at])
             self.ring.start()
 
         def turn(self):
@@ -490,16 +522,19 @@
             self.ring.finish()
             total = self.own[...].astype(F32) + s.minus[self.at].astype(F32)
             self.own[...] = (total + s.plus[self.at].astype(F32)).astype(LOW)
-            self.ring_b.start()
+            (start(self.cells) if self.direct else self.ring_b.start())
 
         def turn_b(self):
             self.ring_b.turn()
 
-        def after_ring_b(self):
-            s = self.set
-            self.ring_b.finish()
-            total = self.own_b[...].astype(F32) + s.minus_b[self.at].astype(F32)
-            total = total + s.plus_b[self.at].astype(F32)
+        def after_cells(self):
+            if self.direct:
+                wait(self.cells)
+            else:
+                self.ring_b.finish()
+            total = self.cell[...].astype(F32)
+            for came in self.cells_in if self.direct else self.cells_in[1:]:
+                total = total + came[...].astype(F32)
             if self.unit < EXPERT_UNITS:
                 expert_out[self.unit] = total
             else:
@@ -515,17 +550,17 @@
                     query_out[:, lane_block((y_at + 4 - off) % 4, 256)] = rows
             for came in self.last_in:
                 total = total + came[...]
-            if self.unit == KEY_UNIT:
-                key_out[...] = total
-            elif self.unit == VALUE_UNIT:
-                value_out[...] = total
+            if self.unit in (KV_UNIT, KV_UNIT + 1):
+                lanes = lane_block(self.unit - KV_UNIT, 256)
+                key_out[:, lanes] = total[:, 0:256]
+                value_out[:, lanes] = total[:, 256:]
             elif self.set is Wide:
                 out_out[:, half[self.unit - OUT_UNIT]] = total
             else:
                 misc_out[...] = total[:, 256:]
 
     extras = {}
-    stages = (Unit.after_pair, Unit.turn, Unit.after_ring, Unit.turn_b, Unit.after_ring_b, Unit.finish)
+    stages = (Unit.after_pair, Unit.turn, Unit.after_ring, Unit.after_cells, Unit.finish, Unit.turn_b)
     units = [Unit(unit) for unit in range(UNITS + 1)]
 
     def run(point):
@@ -548,7 +583,10 @@
             run(point + at)
 
     expert_units(0, 0)
-    loop(2 * OWN_EXPERTS - 2, lambda step: expert_back(step + 2))
+    loop(2, lambda step: expert_back(step + 2))
+    run(26)
+    loop(2, lambda step: expert_back(step + 4))
+    run(27)
 
     dots_copies = [y_copy(off, dots_send.at[(y_at + off) % 4], dots_in.at[off - 1]) for off in (1, 3, 2)]
     for block in range(4):
@@ -610,6 +648,7 @@
     mix_back = Scatter(
         y_at, y_copy, lambda block, part: x_all.at[block, pl.ds(64 * part, 64)], lambda at, part: mix_in.at[at, pl.ds(64 * part, 64)]
     )
+    mix_back.start()
     taken = dots_send[y_at]
     moe_grad = own_row[...]
     for off in (1, 2, 3):
@@ -645,6 +684,8 @@
         weight_grad(OUT_UNIT + part, x_t.at[:, pl.ds(0, 128)], lambda: joined[:, half[part]])
     run(14)
 
+    extras[0] = mix_back.turn
+
     key_sums, value_sums = pair_in.at[0], pair_in.at[3]
     def attend_back(c):
         heads = head_ref(c)[...]
@@ -661,16 +702,19 @@
         q_low[:, lane_block(2 * c)] = turn(first, own_cosine, own_sine, -1.0).astype(LOW)
         q_low[:, lane_block(2 * c + 1)] = turn(second, own_cosine, own_sine, -1.0).astype(LOW)
 
+    def kv_columns(part):
+        lanes = pl.ds(256 * part, 256)
+        return jnp.concatenate([ref[:, :, :, lanes].reshape(512, 256) for ref in (key_sums, value_sums)], axis=1)
+
     for c in range(4):
         attend_back(c)
         run(15 + c)
+        if c % 2 == 1:
+            weight_grad(KV_UNIT + c // 2, normed_t, lambda: kv_columns(c // 2))
+            run(19 + c // 2)
     q_copies = [y_copy(off, q_low.at[:, lane_block(across_block(off), 256)], q_all.at[y_at]) for off in (1, 3, 2)]
     start(q_copies)
     q_all[y_at] = q_low[:, lane_block(y_at, 256)]
-    weight_grad(KEY_UNIT, normed_t, lambda: key_sums[...].reshape(512, WIDE))
-    run(19)
-    weight_grad(VALUE_UNIT, normed_t, lambda: value_sums[...].reshape(512, WIDE))
-    run(20)
 
     for part in (0, 1, 2, 3):
         loads[("bwd", part)].wait()
@@ -682,10 +726,13 @@
         row_send[blocks] = rows.astype(LOW).reshape(2, 128, 1024)
         scaled = rows * normed_all[blocks].reshape(256, 1024).astype(F32)
         gain_rows = gain_rows + jnp.sum(scaled, axis=0, keepdims=True)
+        if part == 0:
+            run(28)
     grad_back = Scatter(
         y_at, y_copy, lambda block, part: row_send.at[block, pl.ds(64 * part, 64)], lambda at, part: grad_in.at[at, pl.ds(64 * part, 64)]
     )
     grad_back.start()
+    run(29)
     rows = dot_nt(q_low[:, 0:WIDE], square(weights, 0)) + dot_nt(q_low[:, WIDE:], square(weights, 1))
     input_grad[...] = rows
     gain_rows = gain_rows + jnp.sum(rows * normed_all[y_at].astype(F32), axis=0, keepdims=True)
@@ -703,7 +750,6 @@
     units[UNITS].begin()
     run(22)
     grad_back.turn()
-    mix_back.start()
     run(23)
 
     grad_back.finish()
@@ -730,7 +776,6 @@
         hidden_out[...] = total
         result(hidden_out, hidden_to)
 
-    extras[0] = mix_back.turn
     extras[1] = finish_mix
     run(24)
     result(expert_out, expert_to)
@@ -753,7 +798,7 @@
         wide(1, 1024), wide(1, 1024), low(EXPERTS, 1024),
         low(SLOT_COUNT, *BIG), low(6, *BIG), low(3, 512, 1024), low(128, 1024), wide(128, 1024), wide(512, 128), wide(512, 128),
         low(4, 128, 1024), low(128, 1024), low(4, 512, 128),
-        low(4, 128, 1024), low(4, 128, 1024), low(4, 128, 1024), low(4, 128, 128),
+        low(4, 128, 1024), low(4, 128, 1024), low(4, 128, 1024), low(4, 16, 128), wide(4, 128, 128),
         low(1024, 512), low(1024, 512), wide(4, 128, 128), wide(512, 128), wide(512, 128),
         wide(4, 16, 128), wide(3, 16, 128), low(4, 128, 1024), low(3, 128, 1024), low(3, 128, 1024),
         low(128, 1024), low(4, 128, 256), low(3, 128, 1024),
@@ -763,7 +808,7 @@
             scratch += [low(1, 4, 4, 2, 32, width)]
         scratch += [low(count, 4, 4, 32, width), low(count, 2, 32, width), low(count, 2, 32, width)]
         scratch += [low(count, 4, 32, width), low(count, 4, 32, width)]
-        scratch += [low(count, 16, width), low(count, 16, width), low(count, 32, width), low(count, 32, width)]
+        scratch += [low(3, count, 32, width)]
         shared = count - EXPERT_UNITS if count == UNITS else 1
         scratch += [wide(shared, 32, width), wide(3, shared, 8, width)]
     scratch += [sems((48,)), sems((48,)), sems((UNITS + 1, 16)), sems((UNITS + 1, 16)), sems((32,))]

time: 115 us -> 109 us (0.948)
  Pallas kernels: 113 us -> 108 us
    pallas_call x1, Pallas kernels: 110 us -> 105 us  [layer(): pl.pallas_call(layer_kernel, out_shape=(shape((128, 1024), F32), shape((1...]
where the time goes in v3:
time: 109 us
  Pallas kernels  108 us (99%)
  between operations  1.36 us (1%)
    pallas_call x1, Pallas kernels, layer(): pl.pallas_call(layer_kernel, out_shape=(shape((128, 1024), F32), shape((1...  105 us
    pallas_call x1, Pallas kernels, place(): pl.pallas_call(place_kernel, out_shape=(shape(128, 1024), shape(128, 1024...  2.68 us

profile of v3, /device:TPU:0, one launch (start us, length us, event | category | flops | bytes accessed | tf_op | source)
XLA Modules:
  0.0 109.3 jit_solution(4995993130458093653)
XLA Ops:
  1.3 105.2 %layer.1 = (f32[128,1024]{1,0:T(8,128)}, f32[128,1024]{1,0:T(8,128)}, f32[9,32,512]{2,1,0:T(8,128)}, f32[8,1024]{1,0:T(8,128)}, f32[8,512]{1,0:T(8,128)}, /*inde...) custom-call(s32[1]{0:T(128)S(6)} %copy.29.prefix, bf16[128,1024]{1,0:T(8,128)(2,1)} %tokens_far.1, ...), custom_call_target="tpu_custom_call" | custom-call | tf_op jit(solution)/shard_map/layer/pallas_call | solution.py:816
  106.5 2.7 %place.1 = (f32[128,1024]{1,0:T(8,128)}, f32[128,1024]{1,0:T(8,128)}, f32[1,8]{1,0:T(1,128)}, f32[8,1024]{1,0:T(8,128)}, f32[8,512]{1,0:T(8,128)}, /*index=5*/f3...) custom-call(f32[128,1024]{1,0:T(8,128)} %get-tuple-element.32.hidden, ...), custom_call_target="tpu_custom_call" | custom-call | tf_op jit(solution)/shard_map/place/pallas_call | solution.py:857

commit v4 on v3

--- a/solution.py
+++ b/solution.py
@@ -27,34 +27,37 @@
     (),
     (),
     ((0, 0),),
-    ((0, 3), (0, 6)),
-    (),
-    (),
+    ((0, 3),),
+    ((0, 6),),
     ((1, 0),),
     (),
     (),
+    ((1, 3),),
+    ((0, 1),),
+    ((1, 6), (0, 4)),
+    ((0, 7), (2, 0), (2, 3), (0, 2), (0, 5), (1, 1)),
+    ((2, 6),),
+    ((0, 8),),
+    ((1, 7), (1, 4), (5, 0)),
+    ((5, 3),),
     (),
-    ((1, 3), (0, 1)),
-    ((1, 6), (0, 4), (0, 7), (2, 0), (0, 2), (0, 5)),
-    ((2, 3), (0, 8)),
-    ((2, 6), (1, 1)),
-    ((1, 4), (1, 7)),
-    ((1, 2),),
-    ((5, 0),),
-    ((0, 11), (5, 3)),
-    (),
-    ((0, 12), (1, 5), (1, 8)),
-    ((2, 1), (2, 4)),
+    ((0, 11),),
+    ((1, 5), (1, 2)),
+    ((0, 12),),
+    ((2, 1),),
     (
-        (0, 10), (1, 11), (1, 12), (2, 7), (2, 2), (0, 13), (1, 9), (3, 0), (3, 3), (2, 5), (2, 8), (1, 10),
-        (5, 1), (5, 4), (3, 6),
+        (0, 10), (1, 12), (1, 11), (6, 0), (2, 7), (1, 9), (2, 4), (2, 5), (0, 13), (2, 2), (3, 0), (3, 3), (5, 1),
+        (2, 8), (3, 6),
     ),
-    ((2, 12), (2, 11), (1, 13), (5, 7), (5, 2), (2, 10), (5, 5), (2, 9), (3, 1)),
-    ((3, 11), (5, 8), (3, 12), (2, 13), (3, 9), (3, 10), (3, 7), (3, 4), (3, 13), (3, 5), (3, 2), (3, 8)),
-    ((6, 1), (4, 11), (4, 12), (4, 9), (4, 10), (4, 13)),
+    ((1, 10), (2, 9), (2, 11), (1, 13), (2, 12), (5, 4), (5, 7), (5, 5)),
+    (
+        (2, 10), (3, 9), (2, 13), (3, 12), (3, 11), (3, 10), (5, 2), (5, 8), (3, 13), (3, 1), (3, 4), (3, 7),
+        (3, 5), (3, 2), (3, 8),
+    ),
+    ((6, 1), (4, 9), (4, 12), (4, 11), (4, 10), (4, 13)),
     (),
     (),
-    ((6, 0), (5, 6)),
+    ((5, 6), (1, 8)),
     ((0, 9),),
 )
 
@@ -439,7 +442,6 @@
     stand(x_all, x_t)
     g_share.near()
     g_share.finish()
-    stand(g_all, g_t)
     loop(2, expert_back)
 
     class Wide:
@@ -579,6 +581,8 @@
 
     def expert_units(j, point):
         for at, (kind, turned_rows) in enumerate(((0, x_t), (3, x_t), (6, g_t))):
+            if kind + j == 6:
+                stand(g_all, g_t)
             weight_grad(kind + j, turned_rows, slab_value(kind + j))
             run(point + at)
 
@@ -619,12 +623,12 @@
     rows_back.near[1].start()
     own_row[...] = rows[128:256]
     run(4)
-    rows_back.turn()
     load_pair("bwd", 4, wo_far, weights, 3)
     load_pair("bwd", 2, wq_far, weights, 0)
     load_keys("bwd", weights, 2, 5)
 
     expert_units(1, 5)
+    rows_back.turn()
     expert_units(2, 8)
 
     def mix_part(part):

time: 109 us -> 107 us (0.982)
  Pallas kernels: 108 us -> 105 us
    pallas_call x1, Pallas kernels: 105 us -> 103 us  [layer(): pl.pallas_call(layer_kernel, out_shape=(shape((128, 1024), F32), shape((1...]
where the time goes in v4:
time: 107 us
  Pallas kernels  105 us (98%)
  between operations  1.36 us (1%)
    pallas_call x1, Pallas kernels, layer(): pl.pallas_call(layer_kernel, out_shape=(shape((128, 1024), F32), shape((1...  103 us
    pallas_call x1, Pallas kernels, place(): pl.pallas_call(place_kernel, out_shape=(shape(128, 1024), shape(128, 1024...  2.68 us

profile of v4, /device:TPU:0, one launch (start us, length us, event | category | flops | bytes accessed | tf_op | source)
XLA Modules:
  0.0 106.6 jit_solution(10479629433702480198)
XLA Ops:
  1.3 102.6 %layer.1 = (f32[128,1024]{1,0:T(8,128)}, f32[128,1024]{1,0:T(8,128)}, f32[9,32,512]{2,1,0:T(8,128)}, f32[8,1024]{1,0:T(8,128)}, f32[8,512]{1,0:T(8,128)}, /*inde...) custom-call(s32[1]{0:T(128)S(6)} %copy.29.prefix, bf16[128,1024]{1,0:T(8,128)(2,1)} %tokens_far.1, ...), custom_call_target="tpu_custom_call" | custom-call | tf_op jit(solution)/shard_map/layer/pallas_call | solution.py:820
  103.9 2.7 %place.1 = (f32[128,1024]{1,0:T(8,128)}, f32[128,1024]{1,0:T(8,128)}, f32[1,8]{1,0:T(1,128)}, f32[8,1024]{1,0:T(8,128)}, f32[8,512]{1,0:T(8,128)}, /*index=5*/f3...) custom-call(f32[128,1024]{1,0:T(8,128)} %get-tuple-element.32.hidden, ...), custom_call_target="tpu_custom_call" | custom-call | tf_op jit(solution)/shard_map/place/pallas_call | solution.py:861

commit v5 on v4

--- a/solution.py
+++ b/solution.py
@@ -585,6 +585,8 @@
                 stand(g_all, g_t)
             weight_grad(kind + j, turned_rows, slab_value(kind + j))
             run(point + at)
+            if kind + j == 4:
+                rows_back.turn()
 
     expert_units(0, 0)
     loop(2, lambda step: expert_back(step + 2))
@@ -628,7 +630,6 @@
     load_keys("bwd", weights, 2, 5)
 
     expert_units(1, 5)
-    rows_back.turn()
     expert_units(2, 8)
 
     def mix_part(part):

time: 107 us -> 107 us (level)
  no operation moved by 1% of the time
where the time goes in v5:
time: 107 us; the launch traced here: 106 us
  Pallas kernels  105 us (98%)
  between operations  1.36 us (1%)
    pallas_call x1, Pallas kernels, layer(): pl.pallas_call(layer_kernel, out_shape=(shape((128, 1024), F32), shape((1...  102 us
    pallas_call x1, Pallas kernels, place(): pl.pallas_call(place_kernel, out_shape=(shape(128, 1024), shape(128, 1024...  2.68 us

profile of v5, /device:TPU:0, one launch (start us, length us, event | category | flops | bytes accessed | tf_op | source)
XLA Modules:
  0.0 106.5 jit_solution(14826513237766879464)
XLA Ops:
  1.3 102.4 %layer.1 = (f32[128,1024]{1,0:T(8,128)}, f32[128,1024]{1,0:T(8,128)}, f32[9,32,512]{2,1,0:T(8,128)}, f32[8,1024]{1,0:T(8,128)}, f32[8,512]{1,0:T(8,128)}, /*inde...) custom-call(s32[1]{0:T(128)S(6)} %copy.29.prefix, bf16[128,1024]{1,0:T(8,128)(2,1)} %tokens_far.1, ...), custom_call_target="tpu_custom_call" | custom-call | tf_op jit(solution)/shard_map/layer/pallas_call | solution.py:821
  103.7 2.7 %place.1 = (f32[128,1024]{1,0:T(8,128)}, f32[128,1024]{1,0:T(8,128)}, f32[1,8]{1,0:T(1,128)}, f32[8,1024]{1,0:T(8,128)}, f32[8,512]{1,0:T(8,128)}, /*index=5*/f3...) custom-call(f32[128,1024]{1,0:T(8,128)} %get-tuple-element.32.hidden, ...), custom_call_target="tpu_custom_call" | custom-call | tf_op jit(solution)/shard_map/place/pallas_call | solution.py:862
